TPU v7x, 128 devices: a whole 4x4x4 slice. The times are simulated.
128 devices in a mesh: row: 16 (over z, x), col: 8 (over y, core).
Axes of the slice: x: 4, y: 4, z: 4, core: 2. Of those that a mesh axis runs over, the one named last changes fastest.
Arguments:
- front_tiles: float32 [2, 16, 256, 4, 8, 256], P(None, 'row', None, None, 'col'), as said below
- child_tiles: float32 [16, 8, 16, 256, 256], P('row', 'col'), may hold values from -4 to 4
- child_target: int32 [16, 8, 16, 2], P('row', 'col'), may hold values from 0 to 31, as said below
- panel_tiles: int32 [2, 2], replicated, may hold values from 0 to 31, as said below
Outputs:
- factored: float32 [2, 16, 256, 4, 8, 256], P(None, 'row', None, None, 'col')
Inputs may be any that keep to these rules, and one draw needn't show every extreme that they name: `child_target`: child tile number d + q of the device in grid row r targets a parent tile row d + 16 * a and a parent tile column (r % 8) + 8 * b, with a < 2 and b < 4. `panel_tiles`: all 4 entries differ. `front_tiles`: with the children's tiles added and all earlier panels' updates applied, every 512 pivot block has a positive diagonal, and the rest of the block has spectral norm under 0.8 times its smallest diagonal entry.
All inputs are finite; a program needn't handle non-finite values.
Results may differ from a plain program's by a relative error of at most 0.0001.
Values sent between devices are 32-bit elements; how exact they have to be, the bound alone decides.
A program may use at most 192 MiB of HBM per device.

v0:
```python
import jax
import jax.numpy as jnp
from jax import lax
from jax.sharding import PartitionSpec as P

PANELS = 2
NEWTON = 7


def newton(pivot_block):
    identity = jnp.eye(pivot_block.shape[0], dtype=jnp.float32)
    estimate = identity / jnp.diagonal(pivot_block)[None, :]
    for iteration in range(NEWTON):
        product = jnp.dot(pivot_block, estimate, precision=lax.Precision.HIGHEST)
        estimate = 2.0 * estimate - jnp.dot(estimate, product, precision=lax.Precision.HIGHEST)
    return estimate


def shards(front_tiles, child_tiles, child_target, panel_tiles):
    row_count = lax.axis_size("row")
    col_count = lax.axis_size("col")
    my_row = lax.axis_index("row")
    my_col = lax.axis_index("col")
    tile_rows = front_tiles.shape[0]
    tile_size = front_tiles.shape[2]
    tile_cols = front_tiles.shape[3]
    matrix = front_tiles.reshape(tile_rows, tile_size, tile_cols, tile_size)
    per_row = child_tiles.shape[2] // row_count
    pieces = child_tiles.reshape(row_count, per_row, tile_size, tile_size)
    targets = child_target.reshape(row_count, per_row, 2)
    landing = (targets[..., 0] // row_count * tile_cols + targets[..., 1] // col_count).astype(
        jnp.float32
    )
    padded_tiles = jnp.zeros((row_count, col_count, per_row, tile_size, tile_size), jnp.float32)
    padded_tiles = lax.dynamic_update_slice_in_dim(
        padded_tiles, pieces[:, None], my_row % col_count, axis=1
    )
    padded_spots = jnp.zeros((row_count, col_count, per_row), jnp.float32)
    padded_spots = lax.dynamic_update_slice_in_dim(
        padded_spots, landing[:, None], my_row % col_count, axis=1
    )
    arrived, arrived_spots = (
        lax.all_to_all(
            padded_tiles.reshape(row_count * col_count, per_row, tile_size, tile_size),
            ("row", "col"),
            split_axis=0,
            concat_axis=0,
            tiled=True,
        ),
        lax.all_to_all(
            padded_spots.reshape(row_count * col_count, per_row),
            ("row", "col"),
            split_axis=0,
            concat_axis=0,
            tiled=True,
        ),
    )
    flattened = arrived.reshape(-1, tile_size * tile_size)
    spot_ids = arrived_spots.reshape(-1).astype(jnp.int32)
    one_hot = (
        spot_ids[None, :] == jnp.arange(tile_rows * tile_cols, dtype=jnp.int32)[:, None]
    ).astype(jnp.float32)
    additions = jnp.dot(one_hot, flattened, precision=lax.Precision.HIGHEST)
    matrix = matrix + additions.reshape(tile_rows, tile_cols, tile_size, tile_size).transpose(
        0, 2, 1, 3
    )
    global_rows = jnp.arange(tile_rows, dtype=jnp.int32) * row_count + my_row
    global_cols = jnp.arange(tile_cols, dtype=jnp.int32) * col_count + my_col
    done_rows = jnp.zeros((tile_rows,), dtype=bool)
    done_cols = jnp.zeros((tile_cols,), dtype=bool)
    for panel_index in range(PANELS):
        chosen = [panel_tiles[panel_index, 0], panel_tiles[panel_index, 1]]
        for pivot_tile in chosen:
            done_rows = done_rows | (global_rows == pivot_tile)
            done_cols = done_cols | (global_cols == pivot_tile)
        column_parts = []
        for pivot_tile in chosen:
            column_piece = lax.dynamic_index_in_dim(
                matrix, pivot_tile // col_count, axis=2, keepdims=False
            )
            column_parts.append(jnp.where(pivot_tile % col_count == my_col, column_piece, 0.0))
        columns = lax.psum(jnp.stack(column_parts, axis=2), "col")
        columns = columns.reshape(tile_rows, tile_size, 2 * tile_size)
        row_parts = []
        diag_parts = []
        for pivot_tile in chosen:
            owned = pivot_tile % row_count == my_row
            row_piece = lax.dynamic_index_in_dim(
                matrix, pivot_tile // row_count, axis=0, keepdims=False
            )
            diag_piece = lax.dynamic_index_in_dim(
                columns, pivot_tile // row_count, axis=0, keepdims=False
            )
            row_parts.append(jnp.where(owned, row_piece, 0.0))
            diag_parts.append(jnp.where(owned, diag_piece, 0.0))
        rows_both, diag_both = lax.psum(
            (jnp.stack(row_parts, axis=0), jnp.stack(diag_parts, axis=0)), "row"
        )
        pivot_block = diag_both.reshape(2 * tile_size, 2 * tile_size)
        upper_rows = rows_both.reshape(2 * tile_size, tile_cols * tile_size)
        column_flat = columns.reshape(tile_rows * tile_size, 2 * tile_size)
        lower_part = jnp.dot(column_flat, newton(pivot_block), precision=lax.Precision.HIGHEST)
        trailing_rows = jnp.repeat(jnp.logical_not(done_rows), tile_size)
        trailing_cols = jnp.repeat(jnp.logical_not(done_cols), tile_size)
        lower_masked = jnp.where(trailing_rows[:, None], lower_part, 0.0)
        upper_masked = jnp.where(trailing_cols[None, :], upper_rows, 0.0)
        flattened_front = matrix.reshape(tile_rows * tile_size, tile_cols * tile_size)
        flattened_front = flattened_front - jnp.dot(
            lower_masked, upper_masked, precision=lax.Precision.HIGHEST
        )
        matrix = flattened_front.reshape(tile_rows, tile_size, tile_cols, tile_size)
        for position, pivot_tile in enumerate(chosen):
            window = slice(position * tile_size, (position + 1) * tile_size)
            new_column = jnp.where(
                trailing_rows[:, None], lower_part[:, window], column_flat[:, window]
            )
            new_column = new_column.reshape(tile_rows, tile_size, tile_size)
            updated = lax.dynamic_update_index_in_dim(
                matrix, new_column, pivot_tile // col_count, axis=2
            )
            matrix = jnp.where(pivot_tile % col_count == my_col, updated, matrix)
    return matrix.reshape(front_tiles.shape)


def solution(mesh):
    in_specs = (
        P(None, "row", None, None, "col", None),
        P("row", "col", None, None, None),
        P("row", "col", None, None),
        P(),
    )
    out_specs = P(None, "row", None, None, "col", None)
    return jax.shard_map(shards, mesh=mesh, in_specs=in_specs, out_specs=out_specs, check_vma=False)
```

profile of v0, /device:TPU:1, one launch (start us, length us, event | category | flops | bytes accessed | tf_op | source)
XLA Modules:
  0.0 1089.9 jit_solution(16815495540190409536)
XLA Ops:
  8.2 11.5 %all-to-all-start = ((f32[128,1,1]{2,1,0:T(1,128)}), f32[128,1,1]{2,1,0:T(1,128)S(1)}, u32[]{:S(2)}, u32[]{:S(2)}) async-start(f32[128,1,1]{2,1,0:T(1,128)} %all_to_all.12), calls=%async_computation | async-start | bytes 131072 | tf_op jit(solution)/shard_map/all_to_all | solution.py:50
  19.8 11.6 %broadcast_in_dim.127 = f32[16,8,1,256,256]{4,3,1,0,2:T(8,128)} broadcast(f32[]{:T(128)} %constant.211.clone.1), dimensions={} | broadcast | bytes 33554436 | tf_op jit(solution)/shard_map/broadcast_in_dim | solution.py:34
  31.4 2.3 bitcast_dynamic-update-slice_fusion
  33.8 10.3 all-to-all-start.1
  49.8 2.4 convert_reduce_fusion
  52.1 469.8 %all-to-all-done.1 = f32[128,1,256,256]{3,2,1,0:T(8,128)} async-done(((f32[128,1,256,256]{3,2,1,0:T(8,128)}), f32[128,1,256,256]{3,2,1,0:T(8,128)}, u32[]{:S(2)}, u32[]{:S(2)}) %all-to-all-start.1) | async-done | bytes 33554464 | tf_op jit(solution)/shard_map/all_to_all | solution.py:43
  522.0 33.8 %copy.25 = f32[128,1,256,256]{0,3,2,1:T(8,128)} copy(f32[128,1,256,256]{3,2,1,0:T(8,128)} %all-to-all-done.1) | data formatting | bytes 67108864 | tf_op jit(solution)/shard_map/reshape | solution.py:58
  555.8 19.6 %bitcast_add_fusion = f32[2,256,4,256]{3,2,1,0:T(4,128)S(1)} fusion(f32[2,1,256,4,1,256]{5,4,3,2,1,0:T(1,128)} %param.4, f32[128,1,256,256]{0,3,2,1:T(8,128)} %copy.25, s32[2,4]{1,0:T(2,128)S(1)} %multiply_add_fusion, s32[128]{0:T(128)S(1)} %convert_reduce_fusion), kind=kOutput, calls=%fused_computation.7 | convolution fusion | flops 805831680 | bytes 37749280 | tf_op jit(solution)/shard_map/dot_general | solution.py:63
  576.5 1.9 pad_maximum_fusion.2
  579.9 1.8 copy.29
  581.6 87.5 %all-reduce.7.cloned.1.call-done = f32[2,256,2,256]{3,2,1,0:T(2,128)} async-done(((f32[2,256,2,256]{3,2,1,0:T(2,128)}), f32[2,256,2,256]{3,2,1,0:T(2,128)}) %all-reduce.7.cloned.1.call-update) | async-done | bytes 1048592 | tf_op jit(solution)/shard_map/psum | solution.py:82
  669.2 2.1 reshape.167
  677.5 2.5 or_not_fusion.1
  680.1 2.5 or_not_fusion
  682.8 1.8 copy.27
  684.6 84.9 %all-reduce.13.cloned.1.call-done = (f32[512,1024]{1,0:T(8,128)}, f32[512,512]{1,0:T(8,128)}) async-done(((f32[512,1024]{1,0:T(8,128)}, f32[512,512]{1,0:T(8,128)}), (f32[512,1024]{1,0:T(8,128)}, f32[512,512]{1,0:T(8,128)})) %all-reduce.13.cloned.1.call-update) | async-done | bytes 3145744 | tf_op jit(solution)/shard_map/psum | solution.py:96
  769.5 8.7 gather_fusion
  778.2 1.8 fusion.20
  780.1 1.8 convolution_subtract_fusion.13
  781.9 1.8 fusion.40
  783.7 1.8 convolution_subtract_fusion.12
  785.6 1.8 fusion.41
  787.5 1.8 convolution_subtract_fusion.11
  789.3 1.8 fusion.42
  791.2 10.6 convolution_subtract_fusion.10
  801.8 1.8 fusion.43
  803.6 1.8 convolution_subtract_fusion.9
  805.5 1.8 fusion.44
  807.4 1.8 convolution_subtract_fusion.8
  809.2 1.8 fusion.45
  811.1 2.3 convolution_subtract_fusion.7
  813.3 1.8 fusion.46
  816.1 1.6 broadcast_in_dim.140
  817.7 6.9 fusion.6
  824.6 2.2 reshape.170
  828.3 10.1 select_n.326
  839.7 7.5 select_n.330
  848.3 1.9 pad_maximum_fusion.4
  851.4 1.8 copy.32
  853.1 57.0 %all-reduce.9.cloned.1.call-done = f32[2,256,2,256]{3,2,1,0:T(2,128)} async-done(((f32[2,256,2,256]{3,2,1,0:T(2,128)}), f32[2,256,2,256]{3,2,1,0:T(2,128)}) %all-reduce.9.cloned.1.call-update) | async-done | bytes 1048592 | tf_op jit(solution)/shard_map/psum | solution.py:82
  910.2 2.1 reshape.172
  913.6 1.8 copy.30
  915.5 95.0 %all-reduce.11.cloned.1.call-done = (f32[512,1024]{1,0:T(8,128)}, f32[512,512]{1,0:T(8,128)}) async-done(((f32[512,1024]{1,0:T(8,128)}, f32[512,512]{1,0:T(8,128)}), (f32[512,1024]{1,0:T(8,128)}, f32[512,512]{1,0:T(8,128)})) %all-reduce.11.cloned.1.call-update) | async-done | bytes 3145744 | tf_op jit(solution)/shard_map/psum | solution.py:96
  1010.4 8.9 gather_fusion.1
  1019.3 1.8 fusion.21
  1021.1 1.8 convolution_subtract_fusion.6
  1022.9 1.8 fusion.47
  1024.8 1.8 convolution_subtract_fusion.5
  1026.7 1.8 fusion.48
  1028.5 1.8 convolution_subtract_fusion.4
  1030.4 1.8 fusion.49
  1032.2 2.1 convolution_subtract_fusion.3
  1034.3 1.8 fusion.50
  1036.2 1.8 convolution_subtract_fusion.2
  1038.0 1.8 fusion.51
  1039.9 1.8 convolution_subtract_fusion.1
  1041.7 1.8 fusion.52
  1043.6 2.1 convolution_subtract_fusion
  1045.7 1.8 fusion.53
  1050.1 6.9 fusion.9
  1057.0 2.2 reshape.175
  1060.6 10.1 select_n.360
  1071.9 7.5 select_n.364
  1079.5 3.5 copy.23
  (58 shorter events, 18.7 us)
Async XLA Ops:
  8.2 25.6 %all-to-all-start = ((f32[128,1,1]{2,1,0:T(1,128)}), f32[128,1,1]{2,1,0:T(1,128)S(1)}, u32[]{:S(2)}, u32[]{:S(2)}) async-start(f32[128,1,1]{2,1,0:T(1,128)} %all_to_all.12), calls=%async_computation | async-start | bytes 131072 | tf_op jit(solution)/shard_map/all_to_all | solution.py:50
  19.8 11.7 %copy-start.2 = (f32[1,1,16,256,256]{4,3,2,1,0:T(8,128)S(1)}, f32[1,1,16,256,256]{4,3,2,1,0:T(8,128)}, u32[]{:S(2)}) copy-start(f32[1,1,16,256,256]{4,3,2,1,0:T(8,128)} %param.5) | copy-start | bytes 12582916
  33.8 10.3 copy-start.5
  33.8 488.2 %all-to-all-start.1 = ((f32[128,1,256,256]{3,2,1,0:T(8,128)}), f32[128,1,256,256]{3,2,1,0:T(8,128)}, u32[]{:S(2)}, u32[]{:S(2)}) async-start(f32[128,1,256,256]{3,2,1,0:T(8,128)} %bitcast.5), calls=%async_computation.1 | async-start | bytes 67108864 | tf_op jit(solution)/shard_map/all_to_all | solution.py:43
  44.0 625.1 %all-reduce.7.cloned.1.call-start = ((), (), s32[]{:S(2)}) async-start(), calls=%async_computation.2 | async-start | bytes 2097152 | tf_op jit(solution)/shard_map/psum | solution.py:82
  578.5 191.1 %all-reduce.13.cloned.1.call-start = ((), (), s32[]{:S(2)}) async-start(), calls=%async_computation.5 | async-start | bytes 6291456 | tf_op jit(solution)/shard_map/psum | solution.py:96
  672.4 237.8 %all-reduce.9.cloned.1.call-start = ((), (), s32[]{:S(2)}) async-start(), calls=%async_computation.3 | async-start | bytes 2097152 | tf_op jit(solution)/shard_map/psum | solution.py:82
  682.7 1.8 copy-start.3
  769.5 8.7 copy-start
  850.2 160.2 %all-reduce.11.cloned.1.call-start = ((), (), s32[]{:S(2)}) async-start(), calls=%async_computation.4 | async-start | bytes 6291456 | tf_op jit(solution)/shard_map/psum | solution.py:96
  913.6 1.8 copy-start.4
  1010.4 8.9 copy-start.1
Sparse Core Ops, SparseCore 0:
  578.6 90.5 all-reduce.6
  672.6 96.8 all-reduce.12
  850.3 59.7 all-reduce.8
  913.5 96.8 all-reduce.10
where the time goes:
time: 1100 us; the launch traced here: 1090 us
  waiting for transfers between devices  794 us (72%)
  local copies, waits for them, and re-layouts  126 us (11%)
  matrix products  98.3 us (9%)
  other arithmetic  24.7 us (2%)
  between operations  24.4 us (2%)
  starting transfers between devices  22.2 us (2%)
    all_to_all x1, waiting for transfers between devices, shards(): lax.all_to_all(padded_tiles.reshape(row_count * col_count, per_row, tile_...  470 us
    psum x2, waiting for transfers between devices, shards(): lax.psum((jnp.stack(row_parts, axis=0), jnp.stack(diag_parts, axis=0)), '...  180 us
    psum x2, waiting for transfers between devices, shards(): columns = lax.psum(jnp.stack(column_parts, axis=2), 'col')  145 us
    select_n x5, local copies, waits for them, and re-layouts, shards(): matrix = jnp.where(pivot_tile % col_count == my_col, updated, matrix)  38.7 us
    dot_general x14, matrix products, newton(): jnp.dot(estimate, product, precision=lax.Precision.HIGHEST)  35.5 us
    reshape x1, local copies, waits for them, and re-layouts, shards(): flattened = arrived.reshape(-1, tile_size * tile_size)  33.8 us
    dot_general x14, matrix products, newton(): product = jnp.dot(pivot_block, estimate, precision=lax.Precision.HIGHEST)  25.8 us
  transfers between devices with their start and end apart: 6, of which 5 were waited for; matrix products, arithmetic and copies ran while one was open for 3% of the time, Pallas kernels for 0%

commit v1 on v0

v1 whole, which is shorter than its diff:
```python
import jax
import jax.numpy as jnp
from jax import lax
from jax.experimental import pallas as pl
from jax.experimental.pallas import tpu as pltpu
from jax.sharding import PartitionSpec as P

MESH = pl.DeviceIdType.MESH
DMA = pltpu.SemaphoreType.DMA
ANY = pl.BlockSpec(memory_space=pl.ANY)
VMEM = pl.BlockSpec(memory_space=pltpu.VMEM)
SMEM = pl.BlockSpec(memory_space=pltpu.SMEM)
F32 = jnp.float32
BF16 = jnp.bfloat16

PLANE = (
    (0, 1), (1, 0), (0, 3), (3, 0), (1, 1), (3, 3), (1, 3), (3, 1),
    (0, 2), (2, 0), (1, 2), (2, 1), (3, 2), (2, 3), (2, 2),
)
COLUMN = ((0, 1), (1, 0), (3, 0), (1, 1), (3, 1), (2, 0), (2, 1))
STEP = (1, 3, 2)
LOOSE_STEPS = 4
TIGHT_STEPS = 2


class Place:
    def __init__(self):
        self.r = lax.axis_index("row")
        self.c = lax.axis_index("col")
        self.z, self.x = self.r // 4, self.r % 4
        self.y, self.k = self.c // 2, self.c % 2

    def row(self, dz, dx):
        return (self.z + dz + 4) % 4 * 4 + (self.x + dx + 4) % 4

    def col(self, dy, dk):
        return (self.y + dy + 4) % 4 * 2 + (self.k + dk + 2) % 2


def remote(src, dst, send, recv, device):
    return pltpu.make_async_remote_copy(
        src_ref=src, dst_ref=dst, send_sem=send, recv_sem=recv, device_id=device, device_id_type=MESH
    )


def greet(me):
    barrier = pltpu.get_barrier_semaphore()
    for dz, dx in PLANE:
        pl.semaphore_signal(barrier, inc=1, device_id=(me.row(dz, dx), me.c), device_id_type=MESH)
    for dy, dk in COLUMN:
        pl.semaphore_signal(barrier, inc=1, device_id=(me.r, me.col(dy, dk)), device_id_type=MESH)
    pl.semaphore_wait(barrier, len(PLANE) + len(COLUMN))


def child_kernel(
    tiles, spots, out, out_spots, mid, mid_spots,
    own_sem, own_spot_sem, send1, recv1, spot_send1, spot_recv1, send2, recv2, spot_send2, spot_recv2,
):
    me = Place()
    greet(me)

    def first(index):
        dz, dx = PLANE[index]
        target = me.row(dz, dx)
        return (
            remote(tiles.at[target], mid.at[me.r], send1.at[index], recv1.at[index], (target, me.c)),
            remote(
                spots, mid_spots.at[me.r], spot_send1.at[index], spot_recv1.at[index], (target, me.c)
            ),
        )

    def second(source, index, tile, spot):
        col = source % 8
        half = source // 8
        place = half * 8 + me.c
        here = (
            pltpu.make_async_copy(tile, out.at[place], own_sem.at[half]),
            pltpu.make_async_copy(spot, out_spots.at[place], own_spot_sem.at[half]),
        )
        there = (
            remote(tile, out.at[place], send2.at[index], recv2.at[place], (me.r, col)),
            remote(spot, out_spots.at[place], spot_send2.at[index], spot_recv2.at[place], (me.r, col)),
        )
        return col, here, there

    def pass_on(source, index, tile, spot):
        col, here, there = second(source, index, tile, spot)

        @pl.when(col == me.c)
        def _():
            for copy in here:
                copy.start()

        @pl.when(col != me.c)
        def _():
            for copy in there:
                copy.start()

    def finish(source, index, tile, spot):
        col, here, there = second(source, index, tile, spot)

        @pl.when(col == me.c)
        def _():
            for copy in here:
                copy.wait()

        @pl.when(col != me.c)
        def _():
            for copy in there:
                copy.wait_send()

    last = len(PLANE)
    for index in range(last):
        for copy in first(index):
            copy.start()
    pass_on(me.r, last, tiles.at[me.r], spots)
    for index, (dz, dx) in enumerate(PLANE):
        source = me.row(-dz, -dx)
        for copy in first(index):
            copy.wait_recv()
        pass_on(source, index, mid.at[source], mid_spots.at[source])
    for index, (dz, dx) in enumerate(PLANE):
        for copy in first(index):
            copy.wait_send()
        source = me.row(-dz, -dx)
        finish(source, index, mid.at[source], mid_spots.at[source])
    finish(me.r, last, tiles.at[me.r], spots)
    for place in range(16):

        @pl.when(me.c != place % 8)
        def _():
            remote(
                out.at[place], out.at[place], send2.at[0], recv2.at[place], (me.r, me.c)
            ).wait_recv()
            remote(
                out_spots.at[place], out_spots.at[place], spot_send2.at[0], spot_recv2.at[place],
                (me.r, me.c),
            ).wait_recv()


def exchange_children(tiles, spots):
    return pl.pallas_call(
        child_kernel,
        name="children",
        out_shape=[
            jax.ShapeDtypeStruct((16, 256, 256), F32),
            jax.ShapeDtypeStruct((16, 8, 128), jnp.int32),
            jax.ShapeDtypeStruct((16, 256, 256), F32),
            jax.ShapeDtypeStruct((16, 8, 128), jnp.int32),
        ],
        in_specs=[ANY, ANY],
        out_specs=[ANY] * 4,
        scratch_shapes=[DMA((2,)), DMA((2,))] + [DMA((16,))] * 8,
        compiler_params=pltpu.CompilerParams(collective_id=0, has_side_effects=True),
    )(tiles, spots)[:2]


def extend_kernel(spots, front, tile, out):
    step = pl.program_id(0)

    @pl.when(step == 0)
    def _():
        out[...] = front[...]

    spot = spots[step]
    out[spot // 4, spot % 4] += tile[0]


def extend_add(spots, front, tiles):
    return pl.pallas_call(
        extend_kernel,
        name="extend",
        out_shape=jax.ShapeDtypeStruct((2, 4, 256, 256), F32),
        grid_spec=pltpu.PrefetchScalarGridSpec(
            num_scalar_prefetch=1,
            grid=(16,),
            in_specs=[
                pl.BlockSpec((2, 4, 256, 256), lambda i, s: (0, 0, 0, 0)),
                pl.BlockSpec((1, 256, 256), lambda i, s: (i, 0, 0)),
            ],
            out_specs=pl.BlockSpec((2, 4, 256, 256), lambda i, s: (0, 0, 0, 0)),
        ),
        compiler_params=pltpu.CompilerParams(vmem_limit_bytes=32 * 2**20),
    )(spots, front, tiles)


def spread_kernel(m, rows, cols, own, row_send, row_recv, col_send, col_recv):
    me = Place()
    greet(me)

    def row_slice(target):
        return m.at[:, :, pl.ds(pl.multiple_of(target * 16, 16), 16), :]

    def col_slice(target):
        return m.at[target // 4, :, pl.ds(pl.multiple_of(target % 4 * 64, 64), 64), :]

    copies = []
    for index, (dz, dx) in enumerate(PLANE):
        target = me.row(dz, dx)
        source = me.row(-dz, -dx)
        sent = remote(row_slice(target), rows.at[me.r], row_send.at[index], row_recv.at[index], (target, me.c))
        sent.start()
        copies.append(sent)
    for index, (dy, dk) in enumerate(COLUMN):
        target = me.col(dy, dk)
        sent = remote(col_slice(target), cols.at[me.c], col_send.at[index], col_recv.at[index], (me.r, target))
        sent.start()
        copies.append(sent)
    mine = (
        pltpu.make_async_copy(row_slice(me.r), rows.at[me.r], own.at[0]),
        pltpu.make_async_copy(col_slice(me.c), cols.at[me.c], own.at[1]),
    )
    for copy in mine:
        copy.start()
    for copy in mine:
        copy.wait()
    for copy in copies:
        copy.wait()


def spread(m):
    return pl.pallas_call(
        spread_kernel,
        name="spread",
        out_shape=[
            jax.ShapeDtypeStruct((16, 2, 4, 16, 256), F32),
            jax.ShapeDtypeStruct((8, 4, 64, 256), F32),
        ],
        in_specs=[ANY],
        out_specs=[ANY] * 2,
        scratch_shapes=[DMA((2,)), DMA((15,)), DMA((15,)), DMA((7,)), DMA((7,))],
        compiler_params=pltpu.CompilerParams(collective_id=1, has_side_effects=True),
    )(m)


class PlaneGather:
    def __init__(self, me, at, own, x_first, sems):
        self.me, self.at, self.own, self.x_first = me, at, own, x_first
        self.send1, self.recv1, self.send2, self.recv2 = sems

    def number(self, one, two):
        return self.me.row(two, one) if self.x_first else self.me.row(one, two)

    def _first(self, index):
        step = STEP[index]
        return lambda source: remote(
            self.own, self.at(source), self.send1.at[index], self.recv1.at[index],
            (self.number(step, 0), self.me.c),
        )

    def _second(self, which, index):
        source = self.number(-STEP[which - 1] if which else 0, 0)
        block = self.at(source)
        slot = which * 3 + index
        return lambda landed: remote(
            block if which else self.own, self.at(landed), self.send2.at[slot], self.recv2.at[slot],
            (self.number(0, STEP[index]), self.me.c),
        )

    def start(self):
        for index in range(3):
            self._first(index)(self.me.r).start()

    def forward(self, which):
        if which:
            source = self.number(-STEP[which - 1], 0)
            self._first(which - 1)(source).wait_recv()
        else:
            source = self.me.r
        for index in range(3):
            self._second(which, index)(source).start()
        return source

    def arrive(self, which, index):
        source = self.number(-STEP[which - 1] if which else 0, -STEP[index])
        self._second(which, index)(source).wait_recv()
        return source

    def drain(self):
        for index in range(3):
            self._first(index)(self.me.r).wait_send()
        for which in range(4):
            for index in range(3):
                self._second(which, index)(self.me.r).wait_send()


def gather_kernel(
    panel, rows, cols, ug, bg, cg, upc, cpc, bsc, bpc, own,
    bs_s, bs_r, bc_s, bc_r, c_s, c_r, cx_s, cx_r, ua, ub, ba, bb, bx_s, bx_r,
):
    me = Place()
    greet(me)
    other = 1 - me.k
    pivots = [panel[j // 2, j % 2] for j in range(4)]
    for j, pivot in enumerate(pivots):
        upc[:, j] = rows[pivot % 16, pivot // 16]
        cpc[j] = cols[pivot % 8, pivot // 8]

    def b_rows(col):
        return upc.at[:, col // 2, pl.ds(pl.multiple_of(col % 2 * 8, 8), 8), :]

    def b_scatter(index):
        dy, dk = COLUMN[index]
        target = me.col(dy, dk)
        return lambda source: remote(
            b_rows(target), bsc.at[source], bs_s.at[index], bs_r.at[index], (me.r, target)
        )

    for index in range(7):
        b_scatter(index)(me.c).start()
    own_scatter = pltpu.make_async_copy(b_rows(me.c), bsc.at[me.c], own.at[0])
    own_scatter.start()

    def u_at(first):
        return lambda source: ug.at[:, pl.ds(first, 2), source]

    u1 = PlaneGather(me, u_at(0), upc.at[:, pl.ds(0, 2)], True, ua)
    u2 = PlaneGather(me, u_at(2), upc.at[:, pl.ds(2, 2)], False, ub)
    u1.start()
    u2.start()
    own_u = pltpu.make_async_copy(upc, ug.at[:, :, me.r], own.at[1])
    own_u.start()

    def c_out(index):
        step = STEP[index]
        return lambda source: remote(
            cpc, cg.at[source], c_s.at[index], c_r.at[index], (me.r, me.col(step, 0))
        )

    def c_swap(which):
        source = me.col(-STEP[which - 1] if which else 0, 0)
        src = cg.at[source] if which else cpc
        return lambda landed: remote(
            src, cg.at[landed], cx_s.at[which], cx_r.at[which], (me.r, me.col(0, 1))
        )

    for index in range(3):
        c_out(index)(me.c).start()
    c_swap(0)(me.c).start()
    own_c = pltpu.make_async_copy(cpc, cg.at[me.c], own.at[2])
    own_c.start()

    own_scatter.wait()
    for index, (dy, dk) in enumerate(COLUMN):
        b_scatter(index)(me.col(-dy, -dk)).wait_recv()
    for j, pivot in enumerate(pivots):
        bpc[j] = bsc[pivot % 8, pivot // 8]

    def b_piece(col):
        return bg.at[:, col // 2, me.r, pl.ds(pl.multiple_of(col % 2 * 8, 8), 8), :]

    def b_gather(index):
        dy, dk = COLUMN[index]
        return lambda source: remote(
            bpc, b_piece(source), bc_s.at[index], bc_r.at[index], (me.r, me.col(dy, dk))
        )

    for index in range(7):
        b_gather(index)(me.c).start()
    own_b = pltpu.make_async_copy(bpc, b_piece(me.c), own.at[3])
    own_b.start()
    own_b.wait()
    for index, (dy, dk) in enumerate(COLUMN):
        b_gather(index)(me.col(-dy, -dk)).wait_recv()

    def b_at(pivot):
        return lambda source: bg.at[:, pivot, source]

    b1 = PlaneGather(me, b_at(me.k), b_at(me.k)(me.r), True, ba)
    b2 = PlaneGather(me, b_at(2 + me.k), b_at(2 + me.k)(me.r), False, bb)
    b1.start()
    b2.start()

    def b_swap(half, slot, source, back):
        pivot = 2 * half + (other if back else me.k)
        block = bg.at[:, pivot, source]
        return remote(block, block, bx_s.at[half, slot], bx_r.at[half, slot], (me.r, me.col(0, 1)))

    for which in range(4):
        for half, gather in enumerate((b1, b2)):
            source = gather.forward(which)
            if which:
                b_swap(half, which - 1, source, False).start()
    for which in range(4):
        for gather in (u1, u2):
            gather.forward(which)
    for which in range(1, 4):
        source = me.col(-STEP[which - 1], 0)
        c_out(which - 1)(source).wait_recv()
        c_swap(which)(source).start()
    for which in range(4):
        for index in range(3):
            for half, gather in enumerate((b1, b2)):
                source = gather.arrive(which, index)
                b_swap(half, 3 + which * 3 + index, source, False).start()

    for which in range(4):
        for index in range(3):
            for gather in (u1, u2):
                gather.arrive(which, index)
    own_u.wait()
    own_c.wait()
    for which in range(4):
        c_swap(which)(me.col(-STEP[which - 1] if which else 0, 1)).wait_recv()
    for half, gather in enumerate((b1, b2)):
        for which in range(1, 4):
            source = gather.number(-STEP[which - 1], 0)
            b_swap(half, which - 1, source, True).wait_recv()
        for which in range(4):
            for index in range(3):
                source = gather.number(-STEP[which - 1] if which else 0, -STEP[index])
                b_swap(half, 3 + which * 3 + index, source, True).wait_recv()
    for index in range(7):
        b_scatter(index)(me.c).wait_send()
        b_gather(index)(me.c).wait_send()
    for index in range(3):
        c_out(index)(me.c).wait_send()
    for which in range(4):
        c_swap(which)(me.c).wait_send()
    for gather in (u1, u2, b1, b2):
        gather.drain()
    for half, gather in enumerate((b1, b2)):
        for slot in range(15):
            b_swap(half, slot, me.r, False).wait_send()


def gather_pivots(panel, rows, cols):
    plane = [DMA((3,)), DMA((3,)), DMA((12,)), DMA((12,))]
    return pl.pallas_call(
        gather_kernel,
        name="gather",
        out_shape=[
            jax.ShapeDtypeStruct((4, 4, 16, 16, 256), F32),
            jax.ShapeDtypeStruct((4, 4, 16, 16, 256), F32),
            jax.ShapeDtypeStruct((8, 4, 64, 256), F32),
        ],
        in_specs=[SMEM, VMEM, VMEM],
        out_specs=[ANY] * 3,
        scratch_shapes=[
            pltpu.VMEM((4, 4, 16, 256), F32),
            pltpu.VMEM((4, 64, 256), F32),
            pltpu.VMEM((8, 4, 8, 256), F32),
            pltpu.VMEM((4, 8, 256), F32),
            DMA((4,)),
            DMA((7,)), DMA((7,)), DMA((7,)), DMA((7,)),
            DMA((3,)), DMA((3,)), DMA((4,)), DMA((4,)),
            plane, plane, plane, plane,
            DMA((2, 15)), DMA((2, 15)),
        ],
        compiler_params=pltpu.CompilerParams(
            collective_id=2, has_side_effects=True, vmem_limit_bytes=32 * 2**20
        ),
    )(panel, rows, cols)


def split(value):
    high = value.astype(BF16)
    return high, (value - high.astype(F32)).astype(BF16)


def dot1(a, b):
    return jnp.dot(a, b, preferred_element_type=F32)


def dot3(a, b):
    return dot1(a[0], b[0]) + (dot1(a[0], b[1]) + dot1(a[1], b[0]))


def invert(block, block_high, block_low, estimate):
    size = block.shape[0]
    diagonal = lax.broadcasted_iota(jnp.int32, (size, size), 0) == lax.broadcasted_iota(
        jnp.int32, (size, size), 1
    )
    value = block[...]
    high, low = split(value)
    block_high[...] = high
    block_low[...] = low
    weights = jnp.sum(jnp.where(diagonal, value, 0.0), axis=0, keepdims=True)
    estimate[...] = jnp.where(diagonal, 1.0 / weights, 0.0)

    def loose(step, carry):
        now = estimate[...]
        high = now.astype(BF16)
        product = dot1(block_high[...], high)
        estimate[...] = 2.0 * now - dot1(high, product.astype(BF16))
        return carry

    def tight(step, carry):
        now = estimate[...]
        halves = split(now)
        product = dot3((block_high[...], block_low[...]), halves)
        estimate[...] = 2.0 * now - dot3(halves, split(product))
        return carry

    lax.fori_loop(0, LOOSE_STEPS, loose, 0)
    lax.fori_loop(0, TIGHT_STEPS, tight, 0)


def factor_kernel(panel, m, ug, bg, cg, out, block, block_high, block_low, x1, x2, l1, l2, c2, lt_high, lt_low):
    r = lax.axis_index("row")
    c = lax.axis_index("col")
    pivots = [panel[j // 2, j % 2] for j in range(4)]
    row_tile = (lax.broadcasted_iota(jnp.int32, (512, 1), 0) // 256) * 16 + r
    in1 = (row_tile == pivots[0]) | (row_tile == pivots[1])
    in2 = (row_tile == pivots[2]) | (row_tile == pivots[3])

    def b_part(rows, cols):
        return jnp.concatenate(
            [bg[2 * cols + j, pl.ds(2 * rows, 2)].reshape(512, 256) for j in range(2)], axis=1
        )

    def c_part(cols):
        return jnp.concatenate([cg[:, 2 * cols + j].reshape(512, 256) for j in range(2)], axis=1)

    block[...] = b_part(0, 0)
    invert(block, block_high, block_low, x1)
    x1_halves = split(x1[...])
    b12 = split(b_part(0, 1))
    t_halves = split(dot3(split(b_part(1, 0)), x1_halves))
    block[...] = b_part(1, 1) - dot3(t_halves, b12)
    lower = dot3(split(c_part(0)), x1_halves)
    l1[...] = lower
    lower = jnp.where(in1, 0.0, lower)
    c2[...] = c_part(1) - dot3(split(lower), b12)
    invert(block, block_high, block_low, x2)
    lower2 = dot3(split(c2[...]), split(x2[...]))
    l2[...] = lower2
    lower2 = jnp.where(in1 | in2, 0.0, lower2)
    halves = split(lower2)
    lt_high[:, 512:], lt_low[:, 512:] = halves
    lt_high[:, :512], lt_low[:, :512] = split(lower - dot3(halves, t_halves))
    for b in range(4):
        update = dot3((lt_high[...], lt_low[...]), split(ug[b].reshape(1024, 256)))
        col_tile = b * 8 + c
        new = m[:, b].reshape(512, 256) - update
        for j in range(4):
            cols = slice(j % 2 * 256, j % 2 * 256 + 256)
            if j < 2:
                column = jnp.where(in1, cg[:, j].reshape(512, 256), l1[:, cols])
            else:
                column = jnp.where(in1 | in2, c2[:, cols], l2[:, cols])
            new = jnp.where(col_tile == pivots[j], column, new)
        out[:, b] = new.reshape(2, 256, 256)


def factor(panel, m, ug, bg, cg):
    square = pltpu.VMEM((512, 512), F32)
    half = pltpu.VMEM((512, 512), BF16)
    return pl.pallas_call(
        factor_kernel,
        name="factor",
        out_shape=jax.ShapeDtypeStruct((2, 4, 256, 256), F32),
        in_specs=[SMEM] + [VMEM] * 4,
        out_specs=VMEM,
        scratch_shapes=[square, half, half] + [square] * 5 + [pltpu.VMEM((512, 1024), BF16)] * 2,
        compiler_params=pltpu.CompilerParams(vmem_limit_bytes=56 * 2**20),
    )(panel, m, ug, bg, cg)


def shards(front_tiles, child_tiles, child_target, panel_tiles):
    front = front_tiles.reshape(2, 256, 4, 256).transpose(0, 2, 1, 3)
    targets = child_target.reshape(16, 2)
    spots = targets[:, 0] // 16 * 4 + targets[:, 1] // 8
    spots = jnp.broadcast_to(jnp.pad(spots, (0, 112)), (8, 128))
    tiles, spot_blocks = exchange_children(child_tiles.reshape(16, 256, 256), spots)
    landed = lax.dynamic_slice_in_dim(spot_blocks[:, 0, :], lax.axis_index("row"), 1, axis=1)[:, 0]
    m = extend_add(landed, front, tiles)
    rows, cols = spread(m)
    ug, bg, cg = gather_pivots(panel_tiles, rows, cols)
    out = factor(panel_tiles, m, ug, bg, cg)
    return out.transpose(0, 2, 1, 3).reshape(front_tiles.shape)


def solution(mesh):
    in_specs = (
        P(None, "row", None, None, "col", None),
        P("row", "col", None, None, None),
        P("row", "col", None, None),
        P(),
    )
    out_specs = P(None, "row", None, None, "col", None)
    return jax.shard_map(shards, mesh=mesh, in_specs=in_specs, out_specs=out_specs, check_vma=False)
```

time: 1100 us -> 234 us (0.21)
  waiting for transfers between devices: 794 us -> 0 us
  Pallas kernels: 0 us -> 210 us
  local copies, waits for them, and re-layouts: 126 us -> 20.9 us
  matrix products: 98.3 us -> 0 us
  between operations: 24.4 us -> 0.09 us
  other arithmetic: 24.7 us -> 0.76 us
  starting transfers between devices: 22.2 us -> 0 us
    all_to_all x2 -> x0, waiting for transfers between devices: 470 us -> none  [the longest x1 470 us: shards(): lax.all_to_all(padded_tiles.reshape(row_count * col_count, per_row, tile_...]
    psum x4 -> x0, waiting for transfers between devices: 324 us -> none  [the longest x2 180 us: shards(): lax.psum((jnp.stack(row_parts, axis=0), jnp.stack(diag_parts, axis=0)), '...]
    pallas_call x0 -> x5, Pallas kernels: none -> 210 us  [the longest x1 72.2 us: exchange_children(): pl.pallas_call(child_kernel, name='children', out_shape=[jax.ShapeDtypeSt...]
    dot_general x33 -> x0, matrix products: 98.3 us -> none  [the longest x14 35.5 us: newton(): jnp.dot(estimate, product, precision=lax.Precision.HIGHEST)]
    select_n x5 -> x0, local copies, waits for them, and re-layouts: 38.7 us -> none  [shards(): matrix = jnp.where(pivot_tile % col_count == my_col, updated, matrix)]
    reshape x5 -> x1, local copies, waits for them, and re-layouts: 42.3 us -> 5.06 us  [shards(): return out.transpose(0, 2, 1, 3).reshape(front_tiles.shape)]
    all_to_all x2 -> x0, starting transfers between devices: 21.8 us -> none  [the longest x1 11.5 us: shards(): lax.all_to_all(padded_spots.reshape(row_count * col_count, per_row), ('ro...]
    gather x2 -> x0, local copies, waits for them, and re-layouts: 17.5 us -> none  [newton(): estimate = identity / jnp.diagonal(pivot_block)[None, :]]
  transfers between devices with their start and end apart: 6 -> 0, of which waited for: 5 -> 0; matrix products, arithmetic and copies ran while one was open for 3% -> 0% of each run, Pallas kernels for 0% -> 0%
where the time goes in v1:
time: 234 us; the launch traced here: 232 us
  Pallas kernels  210 us (90%)
  local copies, waits for them, and re-layouts  20.9 us (9%)
    pallas_call x1, Pallas kernels, exchange_children(): pl.pallas_call(child_kernel, name='children', out_shape=[jax.ShapeDtypeSt...  72.2 us
    pallas_call x1, Pallas kernels, gather_pivots(): pl.pallas_call(gather_kernel, name='gather', out_shape=[jax.ShapeDtypeStr...  67.1 us
    pallas_call x1, Pallas kernels, spread(): pl.pallas_call(spread_kernel, name='spread', out_shape=[jax.ShapeDtypeStr...  40.1 us
    pallas_call x1, Pallas kernels, factor(): pl.pallas_call(factor_kernel, name='factor', out_shape=jax.ShapeDtypeStru...  29.6 us
    unnamed x17, local copies, waits for them, and re-layouts  14 us
    reshape x1, local copies, waits for them, and re-layouts, shards(): return out.transpose(0, 2, 1, 3).reshape(front_tiles.shape)  5.06 us

profile of v1, /device:TPU:1, one launch (start us, length us, event | category | flops | bytes accessed | tf_op | source)
XLA Modules:
  0.0 232.1 jit_solution(8700729526728151750)
XLA Ops:
  0.0 0.8 fusion
  0.8 0.6 broadcast_in_dim.3.spots
  1.4 2.0 copy.10
  3.4 72.2 %children.1 = (f32[16,256,256]{2,1,0:T(8,128)}, s32[16,8,128]{2,1,0:T(8,128)}, f32[16,256,256]{2,1,0:T(8,128)}, s32[16,8,128]{2,1,0:T(8,128)}) custom-call(f32[16,256,256]{2,1,0:T(8,128)} %bitcast.32, s32[8,128]{1,0:T(8,128)} %broadcast_in_dim.3.spots), custom_call_target="tpu_custom_call" | custom-call | tf_op jit(solution)/shard_map/children/pallas_call | solution.py:142
  75.5 0.8 slice.11
  76.4 0.4 dynamic-slice_reduce_fusion.spots
  76.8 0.0 copy-start.1
  76.8 2.2 copy-done.1
  79.0 1.5 extend.1.m
  80.5 0.0 copy-start
  80.5 1.3 copy-done
  81.8 0.0 copy-start.7
  81.8 40.1 %spread.1 = (f32[16,2,4,16,256]{4,3,2,1,0:T(8,128)}, f32[8,4,64,256]{3,2,1,0:T(8,128)}) custom-call(f32[2,4,256,256]{3,2,1,0:T(8,128)} %copy-done), custom_call_target="tpu_custom_call" | custom-call | tf_op jit(solution)/shard_map/spread/pallas_call | solution.py:222
  121.9 0.0 copy-done.7
  121.9 0.0 copy-start.4
  122.0 1.6 copy-done.4
  123.5 0.0 copy-start.5
  123.5 1.6 copy-done.5
  125.1 67.1 %gather.1 = (f32[4,4,16,16,256]{4,3,2,1,0:T(8,128)S(1)}, f32[4,4,16,16,256]{4,3,2,1,0:T(8,128)S(1)}, f32[8,4,64,256]{3,2,1,0:T(8,128)S(1)}) custom-call(s32[2,2]{1,0:T(2,128)S(1)} %copy-done.7, f32[16,2,4,16,256]{4,3,2,1,0:T(8,128)S(1)} %copy-done.4, f32[8,4,64,256]{3,2,1,0:T(8,128)S(1)} %copy-done.5), custom_call_target="tpu_custom_call" | custom-call | tf_op jit(solution)/shard_map/gather/pallas_call | solution.py:429
  192.2 0.0 copy-start.2
  192.2 1.9 copy-done.2
  194.1 0.0 copy-start.3
  194.1 2.0 copy-done.3
  196.1 0.0 copy-start.6
  196.1 1.4 copy-done.6
  197.5 29.6 %factor.1 = f32[2,4,256,256]{3,2,1,0:T(8,128)} custom-call(s32[2,2]{1,0:T(2,128)} %panel.3, f32[2,4,256,256]{3,2,1,0:T(8,128)} %copy-done, f32[4,4,16,16,256]{4,3,2,1,0:T(8,128)} %copy-done.2, f32[4,4,16,16,256]{4,3,2,1,0:T(8,128)} %copy-done.3, f32[8,4,64,256]{3,2,1,0:T(8,128)} %copy-done.6), custom_call_target="tpu_custom_call" | custom-call | tf_op jit(solution)/shard_map/factor/pallas_call | solution.py:549
  227.0 5.1 %copy.8 = f32[2,1,256,4,1,256]{5,4,3,2,1,0:T(1,128)} copy(f32[2,1,256,4,1,256]{5,2,3,0,4,1:T(8,128)} %bitcast.31) | data formatting | bytes 4194304 | tf_op jit(solution)/shard_map/reshape | solution.py:571
  (1 shorter events, 0.0 us)
Async XLA Ops:
  76.8 2.2 copy-start.1
  80.5 1.3 copy-start
  81.8 40.1 %copy-start.7 = (s32[2,2]{1,0:T(2,128)S(1)}, s32[2,2]{1,0:T(2,128)}, u32[]{:S(2)}) copy-start(s32[2,2]{1,0:T(2,128)} %panel.3) | copy-start | bytes 52
  121.9 1.6 copy-start.4
  123.5 1.6 copy-start.5
  192.2 1.9 copy-start.2
  194.1 2.0 copy-start.3
  196.1 1.4 copy-start.6

commit v2 on v1

v2 whole, which is shorter than its diff:
```python
import jax
import jax.numpy as jnp
from jax import lax
from jax.experimental import pallas as pl
from jax.experimental.pallas import tpu as pltpu
from jax.sharding import PartitionSpec as P

MESH = pl.DeviceIdType.MESH
DMA = pltpu.SemaphoreType.DMA
ANY = pl.BlockSpec(memory_space=pl.ANY)
VMEM = pl.BlockSpec(memory_space=pltpu.VMEM)
SMEM = pl.BlockSpec(memory_space=pltpu.SMEM)
F32 = jnp.float32
BF16 = jnp.bfloat16

PLANE = (
    (0, 1), (1, 0), (0, 3), (3, 0), (1, 1), (3, 3), (1, 3), (3, 1),
    (0, 2), (2, 0), (1, 2), (2, 1), (3, 2), (2, 3), (2, 2),
)
COLUMN = ((0, 1), (1, 0), (3, 0), (1, 1), (3, 1), (2, 0), (2, 1))
STEP = (1, 3, 2)
LOOSE_STEPS = 4
TIGHT_STEPS = 2


class Place:
    def __init__(self):
        self.r = lax.axis_index("row")
        self.c = lax.axis_index("col")
        self.z, self.x = self.r // 4, self.r % 4
        self.y, self.k = self.c // 2, self.c % 2

    def row(self, dz, dx):
        return (self.z + dz + 4) % 4 * 4 + (self.x + dx + 4) % 4

    def col(self, dy, dk):
        return (self.y + dy + 4) % 4 * 2 + (self.k + dk + 2) % 2


def remote(src, dst, send, recv, device):
    return pltpu.make_async_remote_copy(
        src_ref=src, dst_ref=dst, send_sem=send, recv_sem=recv, device_id=device, device_id_type=MESH
    )


def greet(me):
    barrier = pltpu.get_barrier_semaphore()
    for dz, dx in PLANE:
        pl.semaphore_signal(barrier, inc=1, device_id=(me.row(dz, dx), me.c), device_id_type=MESH)
    for dy, dk in COLUMN:
        pl.semaphore_signal(barrier, inc=1, device_id=(me.r, me.col(dy, dk)), device_id_type=MESH)
    pl.semaphore_wait(barrier, len(PLANE) + len(COLUMN))


def child_kernel(
    tiles, spots, out, out_spots, mid, mid_spots,
    own_sem, own_spot_sem, send1, recv1, spot_send1, spot_recv1, send2, recv2, spot_send2, spot_recv2,
):
    me = Place()
    greet(me)

    def first(index):
        dz, dx = PLANE[index]
        target = me.row(dz, dx)
        return (
            remote(tiles.at[target], mid.at[me.r], send1.at[index], recv1.at[index], (target, me.c)),
            remote(
                spots, mid_spots.at[me.r], spot_send1.at[index], spot_recv1.at[index], (target, me.c)
            ),
        )

    def second(source, index, tile, spot):
        col = source % 8
        half = source // 8
        place = half * 8 + me.c
        here = (
            pltpu.make_async_copy(tile, out.at[place], own_sem.at[half]),
            pltpu.make_async_copy(spot, out_spots.at[place], own_spot_sem.at[half]),
        )
        there = (
            remote(tile, out.at[place], send2.at[index], recv2.at[place], (me.r, col)),
            remote(spot, out_spots.at[place], spot_send2.at[index], spot_recv2.at[place], (me.r, col)),
        )
        return col, here, there

    def pass_on(source, index, tile, spot):
        col, here, there = second(source, index, tile, spot)

        @pl.when(col == me.c)
        def _():
            for copy in here:
                copy.start()

        @pl.when(col != me.c)
        def _():
            for copy in there:
                copy.start()

    def finish(source, index, tile, spot):
        col, here, there = second(source, index, tile, spot)

        @pl.when(col == me.c)
        def _():
            for copy in here:
                copy.wait()

        @pl.when(col != me.c)
        def _():
            for copy in there:
                copy.wait_send()

    last = len(PLANE)
    for index in range(last):
        for copy in first(index):
            copy.start()
    pass_on(me.r, last, tiles.at[me.r], spots)
    for index, (dz, dx) in enumerate(PLANE):
        source = me.row(-dz, -dx)
        for copy in first(index):
            copy.wait_recv()
        pass_on(source, index, mid.at[source], mid_spots.at[source])
    for index, (dz, dx) in enumerate(PLANE):
        for copy in first(index):
            copy.wait_send()
        source = me.row(-dz, -dx)
        finish(source, index, mid.at[source], mid_spots.at[source])
    finish(me.r, last, tiles.at[me.r], spots)
    for place in range(16):

        @pl.when(me.c != place % 8)
        def _():
            remote(
                out.at[place], out.at[place], send2.at[0], recv2.at[place], (me.r, me.c)
            ).wait_recv()
            remote(
                out_spots.at[place], out_spots.at[place], spot_send2.at[0], spot_recv2.at[place],
                (me.r, me.c),
            ).wait_recv()


def exchange_children(tiles, spots):
    return pl.pallas_call(
        child_kernel,
        name="children",
        out_shape=[
            jax.ShapeDtypeStruct((16, 256, 256), F32),
            jax.ShapeDtypeStruct((16, 8, 128), jnp.int32),
            jax.ShapeDtypeStruct((16, 256, 256), F32),
            jax.ShapeDtypeStruct((16, 8, 128), jnp.int32),
        ],
        in_specs=[ANY, ANY],
        out_specs=[ANY] * 4,
        scratch_shapes=[DMA((2,)), DMA((2,))] + [DMA((16,))] * 8,
        compiler_params=pltpu.CompilerParams(collective_id=0, has_side_effects=True),
    )(tiles, spots)[:2]


def extend_kernel(spots, front, tile, out):
    step = pl.program_id(0)

    @pl.when(step == 0)
    def _():
        for chunk in range(8):
            part = front[pl.ds(chunk, 512, stride=8), :].reshape(2, 256, 128)
            out[:, chunk // 2, :, pl.ds(chunk % 2 * 128, 128)] = part

    spot = spots[step, 0, lax.axis_index("row")]
    out[spot // 4, spot % 4] += tile[0]


def extend_add(spots, front, tiles):
    return pl.pallas_call(
        extend_kernel,
        name="extend",
        out_shape=jax.ShapeDtypeStruct((2, 4, 256, 256), F32),
        grid=(16,),
        in_specs=[SMEM, VMEM, pl.BlockSpec((1, 256, 256), lambda i: (i, 0, 0))],
        out_specs=pl.BlockSpec((2, 4, 256, 256), lambda i: (0, 0, 0, 0)),
        compiler_params=pltpu.CompilerParams(vmem_limit_bytes=32 * 2**20),
    )(spots, front, tiles)


class PlaneGather:
    def __init__(self, me, at, own, x_first, sems):
        self.me, self.at, self.own, self.x_first = me, at, own, x_first
        self.send1, self.recv1, self.send2, self.recv2 = sems

    def number(self, one, two):
        return self.me.row(two, one) if self.x_first else self.me.row(one, two)

    def _first(self, index):
        step = STEP[index]
        return lambda source: remote(
            self.own, self.at(source), self.send1.at[index], self.recv1.at[index],
            (self.number(step, 0), self.me.c),
        )

    def _second(self, which, index):
        source = self.number(-STEP[which - 1] if which else 0, 0)
        block = self.at(source)
        slot = which * 3 + index
        return lambda landed: remote(
            block if which else self.own, self.at(landed), self.send2.at[slot], self.recv2.at[slot],
            (self.number(0, STEP[index]), self.me.c),
        )

    def start(self):
        for index in range(3):
            self._first(index)(self.me.r).start()

    def forward(self, which):
        if which:
            source = self.number(-STEP[which - 1], 0)
            self._first(which - 1)(source).wait_recv()
        else:
            source = self.me.r
        for index in range(3):
            self._second(which, index)(source).start()
        return source

    def arrive(self, which, index):
        source = self.number(-STEP[which - 1] if which else 0, -STEP[index])
        self._second(which, index)(source).wait_recv()
        return source

    def drain(self):
        for index in range(3):
            self._first(index)(self.me.r).wait_send()
        for which in range(4):
            for index in range(3):
                self._second(which, index)(self.me.r).wait_send()


def split(value):
    high = value.astype(BF16)
    return high, (value - high.astype(F32)).astype(BF16)


def dot1(a, b):
    return jnp.dot(a, b, preferred_element_type=F32)


def dot3(a, b):
    return dot1(a[0], b[0]) + (dot1(a[0], b[1]) + dot1(a[1], b[0]))


def invert(block, block_high, block_low, estimate):
    size = block.shape[0]
    diagonal = lax.broadcasted_iota(jnp.int32, (size, size), 0) == lax.broadcasted_iota(
        jnp.int32, (size, size), 1
    )
    value = block[...]
    high, low = split(value)
    block_high[...] = high
    block_low[...] = low
    weights = jnp.sum(jnp.where(diagonal, value, 0.0), axis=0, keepdims=True)
    estimate[...] = jnp.where(diagonal, 1.0 / weights, 0.0)

    def loose(step, carry):
        now = estimate[...]
        high = now.astype(BF16)
        product = dot1(block_high[...], high)
        estimate[...] = 2.0 * now - dot1(high, product.astype(BF16))
        return carry

    def tight(step, carry):
        now = estimate[...]
        halves = split(now)
        product = dot3((block_high[...], block_low[...]), halves)
        estimate[...] = 2.0 * now - dot3(halves, split(product))
        return carry

    lax.fori_loop(0, LOOSE_STEPS, loose, 0)
    lax.fori_loop(0, TIGHT_STEPS, tight, 0)


def pivot_kernel(
    panel, m_in, out, m, rows, cols, ug, bg, cg, upc, cpc, bsc, bpc,
    block, block_high, block_low, x1, x2, l1, l2, c2, lt_high, lt_low, own,
    row_s, row_r, col_s, col_r, bs_s, bs_r, bc_s, bc_r, c_s, c_r, cx_s, cx_r, ua, ub, ba, bb, bx_s, bx_r,
):
    me = Place()
    greet(me)
    pivots = [panel[j // 2, j % 2] for j in range(4)]
    own_m = pltpu.make_async_copy(m_in, m, own.at[6])
    own_m.start()

    def row_slice(target):
        return m_in.at[:, :, pl.ds(pl.multiple_of(target * 16, 16), 16), :]

    def col_slice(target):
        return m_in.at[target // 4, :, pl.ds(pl.multiple_of(target % 4 * 64, 64), 64), :]

    def row_spread(index):
        target = me.row(*PLANE[index])
        return lambda source: remote(
            row_slice(target), rows.at[source], row_s.at[index], row_r.at[index], (target, me.c)
        )

    def col_spread(index):
        target = me.col(*COLUMN[index])
        return lambda source: remote(
            col_slice(target), cols.at[source], col_s.at[index], col_r.at[index], (me.r, target)
        )

    for index in range(15):
        row_spread(index)(me.r).start()
        if index < 7:
            col_spread(index)(me.c).start()
    mine = (
        pltpu.make_async_copy(row_slice(me.r), rows.at[me.r], own.at[0]),
        pltpu.make_async_copy(col_slice(me.c), cols.at[me.c], own.at[1]),
    )
    for copy in mine:
        copy.start()
    for copy in mine:
        copy.wait()
    for index, (dz, dx) in enumerate(PLANE):
        row_spread(index)(me.row(-dz, -dx)).wait_recv()
    for j, pivot in enumerate(pivots):
        upc[:, j] = rows[pivot % 16, pivot // 16]

    def b_rows(col):
        return upc.at[:, col // 2, pl.ds(pl.multiple_of(col % 2 * 8, 8), 8), :]

    def b_scatter(index):
        target = me.col(*COLUMN[index])
        return lambda source: remote(
            b_rows(target), bsc.at[source], bs_s.at[index], bs_r.at[index], (me.r, target)
        )

    for index in range(7):
        b_scatter(index)(me.c).start()
    own_scatter = pltpu.make_async_copy(b_rows(me.c), bsc.at[me.c], own.at[2])
    own_scatter.start()

    def u_at(first):
        return lambda source: ug.at[:, pl.ds(first, 2), source]

    u1 = PlaneGather(me, u_at(0), upc.at[:, pl.ds(0, 2)], True, ua)
    u2 = PlaneGather(me, u_at(2), upc.at[:, pl.ds(2, 2)], False, ub)
    u1.start()
    u2.start()
    own_u = pltpu.make_async_copy(upc, ug.at[:, :, me.r], own.at[3])
    own_u.start()

    own_scatter.wait()
    for index, (dy, dk) in enumerate(COLUMN):
        b_scatter(index)(me.col(-dy, -dk)).wait_recv()
    for j, pivot in enumerate(pivots):
        bpc[j] = bsc[pivot % 8, pivot // 8]

    def b_piece(col):
        return bg.at[:, col // 2, me.r, pl.ds(pl.multiple_of(col % 2 * 8, 8), 8), :]

    def b_gather(index):
        return lambda source: remote(
            bpc, b_piece(source), bc_s.at[index], bc_r.at[index], (me.r, me.col(*COLUMN[index]))
        )

    for index in range(7):
        b_gather(index)(me.c).start()
    own_b = pltpu.make_async_copy(bpc, b_piece(me.c), own.at[4])
    own_b.start()

    for index, (dy, dk) in enumerate(COLUMN):
        col_spread(index)(me.col(-dy, -dk)).wait_recv()
    for j, pivot in enumerate(pivots):
        cpc[j] = cols[pivot % 8, pivot // 8]

    def c_out(index):
        return lambda source: remote(
            cpc, cg.at[source], c_s.at[index], c_r.at[index], (me.r, me.col(STEP[index], 0))
        )

    def c_swap(which):
        source = me.col(-STEP[which - 1] if which else 0, 0)
        src = cg.at[source] if which else cpc
        return lambda landed: remote(
            src, cg.at[landed], cx_s.at[which], cx_r.at[which], (me.r, me.col(0, 1))
        )

    own_b.wait()
    for index, (dy, dk) in enumerate(COLUMN):
        b_gather(index)(me.col(-dy, -dk)).wait_recv()

    def b_at(pivot):
        return lambda source: bg.at[:, pivot, source]

    b1 = PlaneGather(me, b_at(me.k), b_at(me.k)(me.r), True, ba)
    b2 = PlaneGather(me, b_at(2 + me.k), b_at(2 + me.k)(me.r), False, bb)
    b1.start()
    b2.start()

    def b_swap(half, slot, source, back):
        pivot = 2 * half + (1 - me.k if back else me.k)
        block = bg.at[:, pivot, source]
        return remote(block, block, bx_s.at[half, slot], bx_r.at[half, slot], (me.r, me.col(0, 1)))

    for index in range(3):
        c_out(index)(me.c).start()
    c_swap(0)(me.c).start()
    own_c = pltpu.make_async_copy(cpc, cg.at[me.c], own.at[5])
    own_c.start()

    for which in range(4):
        for half, gather in enumerate((b1, b2)):
            source = gather.forward(which)
            if which:
                b_swap(half, which - 1, source, False).start()
    for which in range(4):
        for gather in (u1, u2):
            gather.forward(which)
    for which in range(1, 4):
        source = me.col(-STEP[which - 1], 0)
        c_out(which - 1)(source).wait_recv()
        c_swap(which)(source).start()
    for half, gather in enumerate((b1, b2)):
        for which in range(4):
            for index in range(3):
                source = gather.arrive(which, index)
                b_swap(half, 3 + which * 3 + index, source, False).start()

    def b_arrived(half, gather):
        for which in range(1, 4):
            source = gather.number(-STEP[which - 1], 0)
            b_swap(half, which - 1, source, True).wait_recv()
        for which in range(4):
            for index in range(3):
                source = gather.number(-STEP[which - 1] if which else 0, -STEP[index])
                b_swap(half, 3 + which * 3 + index, source, True).wait_recv()

    row_tile = (lax.broadcasted_iota(jnp.int32, (512, 1), 0) // 256) * 16 + me.r
    in1 = (row_tile == pivots[0]) | (row_tile == pivots[1])
    in2 = (row_tile == pivots[2]) | (row_tile == pivots[3])

    def b_part(rows, cols):
        return jnp.concatenate(
            [bg[2 * cols + j, pl.ds(2 * rows, 2)].reshape(512, 256) for j in range(2)], axis=1
        )

    def c_part(cols):
        return jnp.concatenate([cg[:, 2 * cols + j].reshape(512, 256) for j in range(2)], axis=1)

    b_arrived(0, b1)
    block[...] = b_part(0, 0)
    invert(block, block_high, block_low, x1)
    b_arrived(1, b2)
    x1_halves = split(x1[...])
    b12 = split(b_part(0, 1))
    t_halves = split(dot3(split(b_part(1, 0)), x1_halves))
    block[...] = b_part(1, 1) - dot3(t_halves, b12)
    own_c.wait()
    for which in range(4):
        c_swap(which)(me.col(-STEP[which - 1] if which else 0, 1)).wait_recv()
    lower = dot3(split(c_part(0)), x1_halves)
    l1[...] = lower
    lower = jnp.where(in1, 0.0, lower)
    c2[...] = c_part(1) - dot3(split(lower), b12)
    invert(block, block_high, block_low, x2)
    lower2 = dot3(split(c2[...]), split(x2[...]))
    l2[...] = lower2
    lower2 = jnp.where(in1 | in2, 0.0, lower2)
    halves = split(lower2)
    lt_high[:, 512:], lt_low[:, 512:] = halves
    lt_high[:, :512], lt_low[:, :512] = split(lower - dot3(halves, t_halves))

    own_u.wait()
    own_m.wait()
    for which in range(4):
        for index in range(3):
            for gather in (u1, u2):
                gather.arrive(which, index)
    for b in range(4):
        update = dot3((lt_high[...], lt_low[...]), split(ug[b].reshape(1024, 256)))
        col_tile = b * 8 + me.c
        new = m[:, b].reshape(512, 256) - update
        for j in range(4):
            window = slice(j % 2 * 256, j % 2 * 256 + 256)
            if j < 2:
                column = jnp.where(in1, cg[:, j].reshape(512, 256), l1[:, window])
            else:
                column = jnp.where(in1 | in2, c2[:, window], l2[:, window])
            new = jnp.where(col_tile == pivots[j], column, new)
        for half in range(2):
            out[pl.ds(2 * b + half, 512, stride=8), :] = new[:, half * 128 : half * 128 + 128]

    for index in range(15):
        row_spread(index)(me.r).wait_send()
    for index in range(7):
        col_spread(index)(me.c).wait_send()
        b_scatter(index)(me.c).wait_send()
        b_gather(index)(me.c).wait_send()
    for index in range(3):
        c_out(index)(me.c).wait_send()
    for which in range(4):
        c_swap(which)(me.c).wait_send()
    for gather in (u1, u2, b1, b2):
        gather.drain()
    for half in range(2):
        for slot in range(15):
            b_swap(half, slot, me.r, False).wait_send()


def eliminate(panel, m):
    plane = [DMA((3,)), DMA((3,)), DMA((12,)), DMA((12,))]
    square = pltpu.VMEM((512, 512), F32)
    narrow = pltpu.VMEM((512, 512), BF16)
    return pl.pallas_call(
        pivot_kernel,
        name="pivots",
        out_shape=jax.ShapeDtypeStruct((4096, 128), F32),
        in_specs=[SMEM, ANY],
        out_specs=VMEM,
        scratch_shapes=[
            pltpu.VMEM((2, 4, 256, 256), F32),
            pltpu.VMEM((16, 2, 4, 16, 256), F32),
            pltpu.VMEM((8, 4, 64, 256), F32),
            pltpu.VMEM((4, 4, 16, 16, 256), F32),
            pltpu.VMEM((4, 4, 16, 16, 256), F32),
            pltpu.VMEM((8, 4, 64, 256), F32),
            pltpu.VMEM((4, 4, 16, 256), F32),
            pltpu.VMEM((4, 64, 256), F32),
            pltpu.VMEM((8, 4, 8, 256), F32),
            pltpu.VMEM((4, 8, 256), F32),
            square, narrow, narrow, square, square, square, square, square,
            pltpu.VMEM((512, 1024), BF16), pltpu.VMEM((512, 1024), BF16),
            DMA((7,)),
            DMA((15,)), DMA((15,)), DMA((7,)), DMA((7,)),
            DMA((7,)), DMA((7,)), DMA((7,)), DMA((7,)),
            DMA((3,)), DMA((3,)), DMA((4,)), DMA((4,)),
            plane, plane, plane, plane,
            DMA((2, 15)), DMA((2, 15)),
        ],
        compiler_params=pltpu.CompilerParams(
            collective_id=1, has_side_effects=True, vmem_limit_bytes=56 * 2**20
        ),
    )(panel, m)


def shards(front_tiles, child_tiles, child_target, panel_tiles):
    targets = child_target.reshape(16, 2)
    spots = targets[:, 0] // 16 * 4 + targets[:, 1] // 8
    spots = jnp.broadcast_to(jnp.pad(spots, (0, 112)), (8, 128))
    tiles, landed = exchange_children(child_tiles.reshape(16, 256, 256), spots)
    m = extend_add(landed, front_tiles.reshape(4096, 128), tiles)
    return eliminate(panel_tiles, m).reshape(front_tiles.shape)


def solution(mesh):
    in_specs = (
        P(None, "row", None, None, "col", None),
        P("row", "col", None, None, None),
        P("row", "col", None, None),
        P(),
    )
    out_specs = P(None, "row", None, None, "col", None)
    return jax.shard_map(shards, mesh=mesh, in_specs=in_specs, out_specs=out_specs, check_vma=False)
```

time: 234 us -> 187 us (0.80)
  Pallas kernels: 210 us -> 177 us
  local copies, waits for them, and re-layouts: 20.9 us -> 9.28 us
    pallas_call x3 -> x1, Pallas kernels: 137 us -> 102 us  [eliminate(): pl.pallas_call(pivot_kernel, name='pivots', out_shape=jax.ShapeDtypeStruc...]
    unnamed x17 -> x9, local copies, waits for them, and re-layouts: 14 us -> 8.69 us
    reshape x1 -> x0, local copies, waits for them, and re-layouts: 5.06 us -> none  [shards(): return out.transpose(0, 2, 1, 3).reshape(front_tiles.shape)]
where the time goes in v2:
time: 187 us
  Pallas kernels  177 us (95%)
  local copies, waits for them, and re-layouts  9.28 us (5%)
    pallas_call x1, Pallas kernels, eliminate(): pl.pallas_call(pivot_kernel, name='pivots', out_shape=jax.ShapeDtypeStruc...  102 us
    pallas_call x1, Pallas kernels, exchange_children(): pl.pallas_call(child_kernel, name='children', out_shape=[jax.ShapeDtypeSt...  72 us
    unnamed x9, local copies, waits for them, and re-layouts  8.69 us

profile of v2, /device:TPU:1, one launch (start us, length us, event | category | flops | bytes accessed | tf_op | source)
XLA Modules:
  0.0 187.0 jit_solution(3880676762649310408)
XLA Ops:
  0.0 0.8 fusion
  0.8 0.6 broadcast_in_dim.3.spots
  1.4 0.0 copy-start.2
  1.4 72.0 %children.1 = (f32[16,256,256]{2,1,0:T(8,128)}, s32[16,8,128]{2,1,0:T(8,128)}, f32[16,256,256]{2,1,0:T(8,128)}, s32[16,8,128]{2,1,0:T(8,128)}) custom-call(f32[16,256,256]{2,1,0:T(8,128)} %bitcast.26, s32[8,128]{1,0:T(8,128)} %broadcast_in_dim.3.spots), custom_call_target="tpu_custom_call" | custom-call | tf_op jit(solution)/shard_map/children/pallas_call | solution.py:142
  73.3 0.0 copy-done.2
  73.3 0.0 copy-start.1
  73.4 2.2 %copy-done.1 = f32[16,256,256]{2,1,0:T(8,128)S(1)} copy-done((f32[16,256,256]{2,1,0:T(8,128)S(1)}, f32[16,256,256]{2,1,0:T(8,128)}, u32[]{:S(2)}) %copy-start.1) | copy-done | bytes 4194328
  75.5 0.0 copy-start.3
  75.5 0.8 copy-done.3
  76.4 3.2 %extend.1.m_in = f32[2,4,256,256]{3,2,1,0:T(8,128)S(1)} custom-call(s32[16,8,128]{2,1,0:T(8,128)S(1)} %copy-done.3, f32[4096,128]{1,0:T(8,128)S(1)} %bitcast.24, f32[16,256,256]{2,1,0:T(8,128)S(1)} %copy-done.1), custom_call_target="tpu_custom_call" | custom-call | tf_op jit(solution)/shard_map/extend/pallas_call | solution.py:172
  79.6 0.0 copy-start
  79.6 1.3 copy-done
  80.9 101.7 %pivots.1 = f32[4096,128]{1,0:T(8,128)} custom-call(s32[2,2]{1,0:T(2,128)} %panel.1, f32[2,4,256,256]{3,2,1,0:T(8,128)} %copy-done), custom_call_target="tpu_custom_call" | custom-call | tf_op jit(solution)/shard_map/pivots/pallas_call | solution.py:509
  182.6 4.3 %copy.7 = f32[2,1,256,4,1,256]{5,4,3,2,1,0:T(1,128)} copy(f32[2,1,256,4,1,256]{5,4,3,2,1,0:T(1,128)} %bitcast.25) | data formatting | bytes 4194304
  (1 shorter events, 0.0 us)
Async XLA Ops:
  1.4 72.0 %copy-start.2 = (f32[2,1,256,4,1,256]{5,4,3,2,1,0:T(1,128)S(1)}, f32[2,1,256,4,1,256]{5,4,3,2,1,0:T(1,128)}, u32[]{:S(2)}) copy-start(f32[2,1,256,4,1,256]{5,4,3,2,1,0:T(1,128)} %param.4) | copy-start | bytes 6291460
  73.3 2.2 %copy-start.1 = (f32[16,256,256]{2,1,0:T(8,128)S(1)}, f32[16,256,256]{2,1,0:T(8,128)}, u32[]{:S(2)}) copy-start(f32[16,256,256]{2,1,0:T(8,128)} %get-tuple-element.8.tile) | copy-start | bytes 12582916
  75.5 0.8 copy-start.3
  79.6 1.3 copy-start

commit v3 on v2

v3 whole, which is shorter than its diff:
```python
import jax
import jax.numpy as jnp
from jax import lax
from jax.experimental import pallas as pl
from jax.experimental.pallas import tpu as pltpu
from jax.sharding import PartitionSpec as P

MESH = pl.DeviceIdType.MESH
DMA = pltpu.SemaphoreType.DMA
ANY = pl.BlockSpec(memory_space=pl.ANY)
VMEM = pl.BlockSpec(memory_space=pltpu.VMEM)
SMEM = pl.BlockSpec(memory_space=pltpu.SMEM)
F32 = jnp.float32
BF16 = jnp.bfloat16

SQUARE = tuple((a, (a + s) % 4) for s in (1, 3, 0, 2) for a in (1, 3, 0, 2) if (a, s) != (0, 0))
PLANE = (
    (0, 1), (1, 0), (0, 3), (3, 0), (1, 1), (3, 3), (1, 3), (3, 1),
    (0, 2), (2, 0), (1, 2), (2, 1), (3, 2), (2, 3), (2, 2),
)
COLUMN = ((0, 1), (1, 0), (3, 0), (1, 1), (3, 1), (2, 0), (2, 1))
STEP = (1, 3, 2)
SHIFT = (0, -1, 1, 2)
WINDOW = 6
LOOSE_STEPS = 4
TIGHT_STEPS = 2


class Place:
    def __init__(self):
        self.r = lax.axis_index("row")
        self.c = lax.axis_index("col")
        self.z, self.x = self.r // 4, self.r % 4
        self.y, self.k = self.c // 2, self.c % 2

    def row(self, dz, dx):
        return (self.z + dz + 4) % 4 * 4 + (self.x + dx + 4) % 4

    def col(self, dy, dk):
        return (self.y + dy + 4) % 4 * 2 + (self.k + dk + 2) % 2


def remote(src, dst, send, recv, device):
    return pltpu.make_async_remote_copy(
        src_ref=src, dst_ref=dst, send_sem=send, recv_sem=recv, device_id=device, device_id_type=MESH
    )


def greet(me):
    barrier = pltpu.get_barrier_semaphore()
    for dz, dx in PLANE:
        pl.semaphore_signal(barrier, inc=1, device_id=(me.row(dz, dx), me.c), device_id_type=MESH)
    for dy, dk in COLUMN:
        pl.semaphore_signal(barrier, inc=1, device_id=(me.r, me.col(dy, dk)), device_id_type=MESH)
    pl.semaphore_wait(barrier, len(PLANE) + len(COLUMN))


class Children:
    def __init__(self, me, tiles, spots, mid, mid_spots, landed, landed_spots, sems):
        self.me, self.tiles, self.spots = me, tiles, spots
        self.mid, self.mid_spots, self.landed, self.landed_spots = mid, mid_spots, landed, landed_spots
        (
            self.own, self.own_spot, self.send1, self.recv1, self.spot_send1, self.spot_recv1,
            self.send2, self.recv2, self.spot_send2, self.spot_recv2,
        ) = sems

    def first(self, index):
        target = self.me.row(*SQUARE[index])
        device = (target, self.me.c)
        r = self.me.r
        return (
            remote(self.tiles.at[target], self.mid.at[r], self.send1.at[index], self.recv1.at[index], device),
            remote(
                self.spots, self.mid_spots.at[r], self.spot_send1.at[index], self.spot_recv1.at[index], device
            ),
        )

    def source(self, index):
        if index == len(SQUARE):
            return self.me.r, self.tiles.at[self.me.r], self.spots
        dz, dx = SQUARE[index]
        source = self.me.row(-dz, -dx)
        return source, self.mid.at[source], self.mid_spots.at[source]

    def _second(self, index, away):
        source, tile, spot = self.source(index)
        half = source // 8
        place = half * 8 + self.me.c
        if not away:
            return (
                pltpu.make_async_copy(tile, self.landed.at[place], self.own.at[half]),
                pltpu.make_async_copy(spot, self.landed_spots.at[place], self.own_spot.at[half]),
            )
        device = (self.me.r, source % 8)
        return (
            remote(tile, self.landed.at[place], self.send2.at[index], self.recv2.at[place], device),
            remote(
                spot, self.landed_spots.at[place], self.spot_send2.at[index], self.spot_recv2.at[place], device
            ),
        )

    def pass_on(self, index):
        if index < len(SQUARE):
            for copy in self.first(index):
                copy.wait_recv()
        col = self.source(index)[0] % 8

        @pl.when(col == self.me.c)
        def _():
            for copy in self._second(index, False):
                copy.start()

        @pl.when(col != self.me.c)
        def _():
            for copy in self._second(index, True):
                copy.start()

    def send(self):
        last = len(SQUARE)
        for index in range(last):
            if index == WINDOW:
                self.pass_on(last)
            if index >= WINDOW:
                self.pass_on(index - WINDOW)
            for copy in self.first(index):
                copy.start()
        for index in range(last - WINDOW, last):
            self.pass_on(index)

    def arrive(self, half, dy, dk):
        place = half * 8 + self.me.col(dy, dk)
        tile, spot = self.landed.at[place], self.landed_spots.at[place]
        if (dy, dk) == (0, 0):
            pltpu.make_async_copy(tile, tile, self.own.at[half]).wait()
            pltpu.make_async_copy(spot, spot, self.own_spot.at[half]).wait()
        else:
            device = (self.me.r, self.me.c)
            remote(tile, tile, self.send2.at[0], self.recv2.at[place], device).wait_recv()
            remote(spot, spot, self.spot_send2.at[0], self.spot_recv2.at[place], device).wait_recv()
        return place

    def drain(self):
        for index in range(len(SQUARE) + 1):
            if index < len(SQUARE):
                for copy in self.first(index):
                    copy.wait_send()
            col = self.source(index)[0] % 8

            @pl.when(col != self.me.c)
            def _(index=index):
                for copy in self._second(index, True):
                    copy.wait_send()


class PlaneGather:
    def __init__(self, me, at, own, x_first, relayed, sems):
        self.me, self.at, self.own, self.x_first = me, at, own, x_first
        self.send1, self.recv1, self.send2, self.recv2 = sems
        self.relayed = relayed
        self.near = range(2 if relayed else 3)
        self.far = (2, 3) if relayed else (2,)

    def number(self, one, two):
        return self.me.row(two, one) if self.x_first else self.me.row(one, two)

    def _copy(self, index, own, source, landed, send, recv, targets):
        block, landed = self.at(source) if own is None else own, self.at(landed)
        if self.relayed and index >= 2:
            half = pl.ds(2 * (index - 2), 2)
            block, landed = self.at(source).at[half], landed.at[half]
            index -= 2
        return remote(block, landed, send, recv, (targets[index], self.me.c))

    def _first(self, index, source, landed):
        targets = [self.number(step, 0) for step in (1, -1, 2)]
        return self._copy(
            index, self.own, source, landed, self.send1.at[index], self.recv1.at[index], targets
        )

    def _second(self, which, index, source, landed):
        targets = [self.number(0, step) for step in (1, -1, 2)]
        slot = which * 4 + index
        return self._copy(
            index, None if which else self.own, source, landed,
            self.send2.at[slot], self.recv2.at[slot], targets,
        )

    def start(self):
        for index in self.near:
            self._first(index, self.me.r, self.me.r).start()

    def relay(self):
        for index, shift in enumerate((-1, 1)):
            source = self.number(shift, 0)
            self._first(index, self.me.r, source).wait_recv()
            if self.relayed:
                self._first(index + 2, source, source).start()

    def forward(self, which):
        source = self.number(SHIFT[which], 0)
        if which == 3:
            for index in self.far:
                self._first(index, source, source).wait_recv()
        for index in self.near:
            self._second(which, index, source, source).start()
        return source

    def relay_second(self, which):
        landed = []
        for index, shift in enumerate((-1, 1)):
            source = self.number(SHIFT[which], shift)
            self._second(which, index, source, source).wait_recv()
            if self.relayed:
                self._second(which, index + 2, source, source).start()
            landed.append(source)
        return landed

    def finish(self, which):
        source = self.number(SHIFT[which], 2)
        for index in self.far:
            self._second(which, index, source, source).wait_recv()
        return source

    def drain(self):
        messages = (*range(2), *self.far)
        for index in messages:
            self._first(index, self.me.r, self.me.r).wait_send()
        for which in range(4):
            for index in messages:
                self._second(which, index, self.me.r, self.me.r).wait_send()


def split(value):
    high = value.astype(BF16)
    return high, (value - high.astype(F32)).astype(BF16)


def dot1(a, b):
    return jnp.dot(a, b, preferred_element_type=F32)


def dot3(a, b):
    return dot1(a[0], b[0]) + (dot1(a[0], b[1]) + dot1(a[1], b[0]))


def invert(block, block_high, block_low, estimate):
    size = block.shape[0]
    diagonal = lax.broadcasted_iota(jnp.int32, (size, size), 0) == lax.broadcasted_iota(
        jnp.int32, (size, size), 1
    )
    value = block[...]
    high, low = split(value)
    block_high[...] = high
    block_low[...] = low
    weights = jnp.sum(jnp.where(diagonal, value, 0.0), axis=0, keepdims=True)
    estimate[...] = jnp.where(diagonal, 1.0 / weights, 0.0)

    def loose(step, carry):
        now = estimate[...]
        high = now.astype(BF16)
        product = dot1(block_high[...], high)
        estimate[...] = 2.0 * now - dot1(high, product.astype(BF16))
        return carry

    def tight(step, carry):
        now = estimate[...]
        halves = split(now)
        product = dot3((block_high[...], block_low[...]), halves)
        estimate[...] = 2.0 * now - dot3(halves, split(product))
        return carry

    lax.fori_loop(0, LOOSE_STEPS, loose, 0)
    lax.fori_loop(0, TIGHT_STEPS, tight, 0)


def pivot_kernel(
    panel, targets, front, tiles, out, mid, mid_spots, spots, landed, landed_spots, m, result, rows, cols, ug, bg, cg, upc, cpc, bsc, bpc,
    block, block_high, block_low, x1, x2, l1, l2, c2, lt_high, lt_low, own,
    row_s, row_r, col_s, col_r, bs_s, bs_r, bc_s, bc_r, c_s, c_r, cx_s, cx_r, ua, ub, ba, bb, bx_s, bx_r,
    out_sem, child_sems,
):
    me = Place()
    greet(me)
    pivots = [panel[j // 2, j % 2] for j in range(4)]

    spots[...] = jnp.zeros_like(spots)
    spots[0:1, 0:16] = targets[0:1, :] // 16 * 4 + targets[1:2, :] // 8
    children = Children(me, tiles, spots, mid, mid_spots, landed, landed_spots, child_sems)
    children.send()
    for chunk in range(8):
        part = front[pl.ds(chunk, 512, stride=8), :].reshape(2, 256, 128)
        m[:, chunk // 2, :, pl.ds(chunk % 2 * 128, 128)] = part
    lane = lax.broadcasted_iota(jnp.int32, (8, 128), 1)
    for half in range(2):
        for dy, dk in ((0, 0), *COLUMN):
            place = children.arrive(half, dy, dk)
            spot = jnp.where(lane == me.r, landed_spots[place], 0)
            spot = jnp.sum(spot.astype(F32), keepdims=True).astype(jnp.int32)

            def add(slot, carry, place=place, spot=spot):
                m[slot // 4, slot % 4] += jnp.where(spot == slot, landed[place], 0.0)
                return carry

            lax.fori_loop(0, 8, add, 0)

    def row_slice(target):
        return m.at[:, :, pl.ds(pl.multiple_of(target * 16, 16), 16), :]

    def col_slice(target):
        return m.at[target // 4, :, pl.ds(pl.multiple_of(target % 4 * 64, 64), 64), :]

    def row_spread(index):
        target = me.row(*PLANE[index])
        return lambda source: remote(
            row_slice(target), rows.at[source], row_s.at[index], row_r.at[index], (target, me.c)
        )

    def col_spread(index):
        target = me.col(*COLUMN[index])
        return lambda source: remote(
            col_slice(target), cols.at[source], col_s.at[index], col_r.at[index], (me.r, target)
        )

    for index in range(15):
        row_spread(index)(me.r).start()
        if index < 7:
            col_spread(index)(me.c).start()
    mine = (
        pltpu.make_async_copy(row_slice(me.r), rows.at[me.r], own.at[0]),
        pltpu.make_async_copy(col_slice(me.c), cols.at[me.c], own.at[1]),
    )
    for copy in mine:
        copy.start()
    for copy in mine:
        copy.wait()
    for index, (dz, dx) in enumerate(PLANE):
        row_spread(index)(me.row(-dz, -dx)).wait_recv()
    for j, pivot in enumerate(pivots):
        upc[:, j] = rows[pivot % 16, pivot // 16]

    def b_rows(col):
        return upc.at[:, col // 2, pl.ds(pl.multiple_of(col % 2 * 8, 8), 8), :]

    def b_scatter(index):
        target = me.col(*COLUMN[index])
        return lambda source: remote(
            b_rows(target), bsc.at[source], bs_s.at[index], bs_r.at[index], (me.r, target)
        )

    for index in range(7):
        b_scatter(index)(me.c).start()
    own_scatter = pltpu.make_async_copy(b_rows(me.c), bsc.at[me.c], own.at[2])
    own_scatter.start()

    def u_at(first):
        return lambda source: ug.at[:, pl.ds(first, 2), source]

    u1 = PlaneGather(me, u_at(0), upc.at[:, pl.ds(0, 2)], True, True, ua)
    u2 = PlaneGather(me, u_at(2), upc.at[:, pl.ds(2, 2)], False, True, ub)
    u1.start()
    u2.start()
    own_u = pltpu.make_async_copy(upc, ug.at[:, :, me.r], own.at[3])
    own_u.start()

    own_scatter.wait()
    for index, (dy, dk) in enumerate(COLUMN):
        b_scatter(index)(me.col(-dy, -dk)).wait_recv()
    for j, pivot in enumerate(pivots):
        bpc[j] = bsc[pivot % 8, pivot // 8]

    def b_piece(col):
        return bg.at[:, col // 2, me.r, pl.ds(pl.multiple_of(col % 2 * 8, 8), 8), :]

    def b_gather(index):
        return lambda source: remote(
            bpc, b_piece(source), bc_s.at[index], bc_r.at[index], (me.r, me.col(*COLUMN[index]))
        )

    for index in range(7):
        b_gather(index)(me.c).start()
    own_b = pltpu.make_async_copy(bpc, b_piece(me.c), own.at[4])
    own_b.start()

    for index, (dy, dk) in enumerate(COLUMN):
        col_spread(index)(me.col(-dy, -dk)).wait_recv()
    for j, pivot in enumerate(pivots):
        cpc[j] = cols[pivot % 8, pivot // 8]

    def c_out(index):
        return lambda source: remote(
            cpc, cg.at[source], c_s.at[index], c_r.at[index], (me.r, me.col(STEP[index], 0))
        )

    def c_swap(which):
        source = me.col(-STEP[which - 1] if which else 0, 0)
        src = cg.at[source] if which else cpc
        return lambda landed: remote(
            src, cg.at[landed], cx_s.at[which], cx_r.at[which], (me.r, me.col(0, 1))
        )

    own_b.wait()
    for index, (dy, dk) in enumerate(COLUMN):
        b_gather(index)(me.col(-dy, -dk)).wait_recv()

    def b_at(pivot):
        return lambda source: bg.at[:, pivot, source]

    b1 = PlaneGather(me, b_at(me.k), b_at(me.k)(me.r), True, False, ba)
    b2 = PlaneGather(me, b_at(2 + me.k), b_at(2 + me.k)(me.r), False, False, bb)
    b1.start()
    b2.start()

    def b_swap(half, slot, source, back):
        pivot = 2 * half + (1 - me.k if back else me.k)
        block = bg.at[:, pivot, source]
        return remote(block, block, bx_s.at[half, slot], bx_r.at[half, slot], (me.r, me.col(0, 1)))

    for gather in (b1, b2):
        gather.forward(0)
    for index in range(3):
        c_out(index)(me.c).start()
    c_swap(0)(me.c).start()
    own_c = pltpu.make_async_copy(cpc, cg.at[me.c], own.at[5])
    own_c.start()

    for gather in (u1, u2, b1, b2):
        gather.relay()
    for which in range(1, 4):
        for half, gather in enumerate((b1, b2)):
            source = gather.forward(which)
            b_swap(half, which - 1, source, False).start()
    for which in range(4):
        for gather in (u1, u2):
            gather.forward(which)
    for which in range(4):
        for half, gather in enumerate((b1, b2)):
            for index, source in enumerate(gather.relay_second(which)):
                b_swap(half, 3 + which * 3 + index, source, False).start()
    for which in range(1, 4):
        source = me.col(-STEP[which - 1], 0)
        c_out(which - 1)(source).wait_recv()
        c_swap(which)(source).start()
    for gather in (u1, u2):
        gather.relay_second(0)
    for half, gather in enumerate((b1, b2)):
        for which in range(4):
            source = gather.finish(which)
            b_swap(half, 5 + which * 3, source, False).start()

    def b_arrived(half, gather):
        for which in range(4):
            if which:
                source = gather.number(SHIFT[which], 0)
                b_swap(half, which - 1, source, True).wait_recv()
            for index, shift in enumerate((-1, 1, 2)):
                source = gather.number(SHIFT[which], shift)
                b_swap(half, 3 + which * 3 + index, source, True).wait_recv()

    def u_relay(which):
        for gather in (u1, u2):
            gather.relay_second(which)

    row_tile = (lax.broadcasted_iota(jnp.int32, (512, 1), 0) // 256) * 16 + me.r
    in1 = (row_tile == pivots[0]) | (row_tile == pivots[1])
    in2 = (row_tile == pivots[2]) | (row_tile == pivots[3])

    def b_part(rows, cols):
        return jnp.concatenate(
            [bg[2 * cols + j, pl.ds(2 * rows, 2)].reshape(512, 256) for j in range(2)], axis=1
        )

    def c_part(cols):
        return jnp.concatenate([cg[:, 2 * cols + j].reshape(512, 256) for j in range(2)], axis=1)

    b_arrived(0, b1)
    block[...] = b_part(0, 0)
    u_relay(1)
    invert(block, block_high, block_low, x1)
    b_arrived(1, b2)
    u_relay(2)
    x1_halves = split(x1[...])
    b12 = split(b_part(0, 1))
    t_halves = split(dot3(split(b_part(1, 0)), x1_halves))
    block[...] = b_part(1, 1) - dot3(t_halves, b12)
    u_relay(3)
    own_c.wait()
    for which in range(4):
        c_swap(which)(me.col(-STEP[which - 1] if which else 0, 1)).wait_recv()
    lower = dot3(split(c_part(0)), x1_halves)
    l1[...] = lower
    lower = jnp.where(in1, 0.0, lower)
    c2[...] = c_part(1) - dot3(split(lower), b12)
    invert(block, block_high, block_low, x2)
    lower2 = dot3(split(c2[...]), split(x2[...]))
    l2[...] = lower2
    lower2 = jnp.where(in1 | in2, 0.0, lower2)
    halves = split(lower2)
    lt_high[:, 512:], lt_low[:, 512:] = halves
    lt_high[:, :512], lt_low[:, :512] = split(lower - dot3(halves, t_halves))

    own_u.wait()
    for which in range(4):
        for gather in (u1, u2):
            gather.finish(which)
    for b in range(4):
        update = dot3((lt_high[...], lt_low[...]), split(ug[b].reshape(1024, 256)))
        col_tile = b * 8 + me.c
        new = m[:, b].reshape(512, 256) - update
        for j in range(4):
            window = slice(j % 2 * 256, j % 2 * 256 + 256)
            if j < 2:
                column = jnp.where(in1, cg[:, j].reshape(512, 256), l1[:, window])
            else:
                column = jnp.where(in1 | in2, c2[:, window], l2[:, window])
            new = jnp.where(col_tile == pivots[j], column, new)
        for half in range(2):
            result[pl.ds(2 * b + half, 512, stride=8), :] = new[:, half * 128 : half * 128 + 128]

    written = [
        pltpu.make_async_copy(result.at[pl.ds(512 * i, 512)], out.at[pl.ds(512 * i, 512)], out_sem.at[i])
        for i in range(8)
    ]
    for copy in written:
        copy.start()
    children.drain()
    for index in range(15):
        row_spread(index)(me.r).wait_send()
    for index in range(7):
        col_spread(index)(me.c).wait_send()
        b_scatter(index)(me.c).wait_send()
        b_gather(index)(me.c).wait_send()
    for index in range(3):
        c_out(index)(me.c).wait_send()
    for which in range(4):
        c_swap(which)(me.c).wait_send()
    for gather in (u1, u2, b1, b2):
        gather.drain()
    for half in range(2):
        for slot in range(15):
            b_swap(half, slot, me.r, False).wait_send()
    for copy in written:
        copy.wait()


def eliminate(panel, targets, front, tiles):
    plane = [DMA((4,)), DMA((4,)), DMA((16,)), DMA((16,))]
    square = pltpu.VMEM((512, 512), F32)
    narrow = pltpu.VMEM((512, 512), BF16)
    return pl.pallas_call(
        pivot_kernel,
        name="pivots",
        out_shape=[
            jax.ShapeDtypeStruct((4096, 128), F32),
            jax.ShapeDtypeStruct((16, 256, 256), F32),
            jax.ShapeDtypeStruct((16, 8, 128), jnp.int32),
        ],
        in_specs=[SMEM, VMEM, VMEM, ANY],
        out_specs=[ANY] * 3,
        scratch_shapes=[
            pltpu.VMEM((8, 128), jnp.int32),
            pltpu.VMEM((16, 256, 256), F32),
            pltpu.VMEM((16, 8, 128), jnp.int32),
            pltpu.VMEM((2, 4, 256, 256), F32),
            pltpu.VMEM((4096, 128), F32),
            pltpu.VMEM((16, 2, 4, 16, 256), F32),
            pltpu.VMEM((8, 4, 64, 256), F32),
            pltpu.VMEM((4, 4, 16, 16, 256), F32),
            pltpu.VMEM((4, 4, 16, 16, 256), F32),
            pltpu.VMEM((8, 4, 64, 256), F32),
            pltpu.VMEM((4, 4, 16, 256), F32),
            pltpu.VMEM((4, 64, 256), F32),
            pltpu.VMEM((8, 4, 8, 256), F32),
            pltpu.VMEM((4, 8, 256), F32),
            square, narrow, narrow, square, square, square, square, square,
            pltpu.VMEM((512, 1024), BF16), pltpu.VMEM((512, 1024), BF16),
            DMA((7,)),
            DMA((15,)), DMA((15,)), DMA((7,)), DMA((7,)),
            DMA((7,)), DMA((7,)), DMA((7,)), DMA((7,)),
            DMA((3,)), DMA((3,)), DMA((4,)), DMA((4,)),
            plane, plane, plane, plane,
            DMA((2, 15)), DMA((2, 15)),
            DMA((8,)), [DMA((2,)), DMA((2,))] + [DMA((16,))] * 8,
        ],
        compiler_params=pltpu.CompilerParams(
            collective_id=0, has_side_effects=True, vmem_limit_bytes=56 * 2**20
        ),
    )(panel, targets, front, tiles)[0]


def hand_over_kernel(source, out, sems):
    copies = [
        pltpu.make_async_copy(source.at[pl.ds(512 * i, 512)], out.at[pl.ds(512 * i, 512)], sems.at[i])
        for i in range(8)
    ]
    for copy in copies:
        copy.start()
    for copy in copies:
        copy.wait()


def hand_over(result):
    return pl.pallas_call(
        hand_over_kernel,
        name="hand_over",
        out_shape=jax.ShapeDtypeStruct(result.shape, result.dtype),
        in_specs=[VMEM],
        out_specs=ANY,
        scratch_shapes=[DMA((8,))],
    )(result)


def shards(front_tiles, child_tiles, child_target, panel_tiles):
    result = eliminate(
        panel_tiles,
        child_target.reshape(16, 2).T,
        front_tiles.reshape(4096, 128),
        child_tiles.reshape(16, 256, 256),
    )
    return hand_over(result).reshape(front_tiles.shape)


def solution(mesh):
    in_specs = (
        P(None, "row", None, None, "col", None),
        P("row", "col", None, None, None),
        P("row", "col", None, None),
        P(),
    )
    out_specs = P(None, "row", None, None, "col", None)
    return jax.shard_map(shards, mesh=mesh, in_specs=in_specs, out_specs=out_specs, check_vma=False)
```

time: 187 us -> 163 us (0.87)
  Pallas kernels: 177 us -> 162 us
  local copies, waits for them, and re-layouts: 9.28 us -> 0 us
    pallas_call x3 -> x2, Pallas kernels: 177 us -> 162 us  [the longest x1 159 us: eliminate(): pl.pallas_call(pivot_kernel, name='pivots', out_shape=[jax.ShapeDtypeStru...]
    unnamed x9 -> x0, local copies, waits for them, and re-layouts: 8.69 us -> none
where the time goes in v3:
time: 163 us; the launch traced here: 162 us
  Pallas kernels  162 us (99%)
    pallas_call x1, Pallas kernels, eliminate(): pl.pallas_call(pivot_kernel, name='pivots', out_shape=[jax.ShapeDtypeStru...  159 us

profile of v3, /device:TPU:1, one launch (start us, length us, event | category | flops | bytes accessed | tf_op | source)
XLA Modules:
  0.0 162.4 jit_solution(534784414770514274)
XLA Ops:
  0.0 159.3 %pivots.1 = (f32[4096,128]{1,0:T(8,128)}, f32[16,256,256]{2,1,0:T(8,128)}, s32[16,8,128]{2,1,0:T(8,128)}) custom-call(s32[2,2]{1,0:T(2,128)} %panel.1, s32[2,16]{1,0:T(2,128)} %bitcast.8, f32[4096,128]{1,0:T(8,128)} %bitcast.7, f32[16,256,256]{2,1,0:T(8,128)} %bitcast.6), custom_call_target="tpu_custom_call" | custom-call | tf_op jit(solution)/shard_map/pivots/pallas_call | solution.py:549
  159.3 3.0 %hand_over.1 = f32[4096,128]{1,0:T(8,128)} custom-call(f32[4096,128]{1,0:T(8,128)} %get-tuple-element.6.source), custom_call_target="tpu_custom_call" | custom-call | tf_op jit(solution)/shard_map/hand_over/pallas_call | solution.py:602

commit v4 on v3

--- a/solution.py
+++ b/solution.py
@@ -22,8 +22,7 @@
 STEP = (1, 3, 2)
 SHIFT = (0, -1, 1, 2)
 WINDOW = 6
-LOOSE_STEPS = 4
-TIGHT_STEPS = 2
+LOOSE_STEPS = 3
 
 
 class Place:
@@ -127,6 +126,18 @@
         for index in range(last - WINDOW, last):
             self.pass_on(index)
 
+    def first_half(self):
+        def rank(value):
+            return jnp.where(value == 1, 0, jnp.where(value == 3, 1, jnp.where(value == 0, 2, 3)))
+
+        steps = []
+        for half in range(2):
+            source = self.me.c + 8 * half
+            dz, dx = (self.me.z - source // 4 + 4) % 4, (self.me.x - source % 4 + 4) % 4
+            step = 4 * rank((dx - dz + 4) % 4) + rank(dz)
+            steps.append(jnp.where(source == self.me.r, -1, step))
+        return jnp.where(steps[0] < steps[1], 0, 1)
+
     def arrive(self, half, dy, dk):
         place = half * 8 + self.me.col(dy, dk)
         tile, spot = self.landed.at[place], self.landed_spots.at[place]
@@ -249,11 +260,11 @@
         jnp.int32, (size, size), 1
     )
     value = block[...]
-    high, low = split(value)
-    block_high[...] = high
-    block_low[...] = low
-    weights = jnp.sum(jnp.where(diagonal, value, 0.0), axis=0, keepdims=True)
-    estimate[...] = jnp.where(diagonal, 1.0 / weights, 0.0)
+    block_high[...], block_low[...] = split(value)
+    weights = jnp.where(diagonal, value, 0.0)
+    by_row = 1.0 / jnp.sum(weights, axis=1, keepdims=True)
+    by_col = 1.0 / jnp.sum(weights, axis=0, keepdims=True)
+    estimate[...] = jnp.where(diagonal, by_col, -(by_row * value * by_col))
 
     def loose(step, carry):
         now = estimate[...]
@@ -262,15 +273,16 @@
         estimate[...] = 2.0 * now - dot1(high, product.astype(BF16))
         return carry
 
-    def tight(step, carry):
-        now = estimate[...]
-        halves = split(now)
-        product = dot3((block_high[...], block_low[...]), halves)
-        estimate[...] = 2.0 * now - dot3(halves, split(product))
-        return carry
+    def residual(halves):
+        return jnp.where(diagonal, 1.0, 0.0) - dot3((block_high[...], block_low[...]), halves)
 
     lax.fori_loop(0, LOOSE_STEPS, loose, 0)
-    lax.fori_loop(0, TIGHT_STEPS, tight, 0)
+    now = estimate[...]
+    halves = split(now)
+    estimate[...] = now + dot1(halves[0], residual(halves).astype(BF16))
+    now = estimate[...]
+    halves = split(now)
+    estimate[...] = now + dot3(halves, split(residual(halves)))
 
 
 def pivot_kernel(
@@ -291,14 +303,18 @@
         part = front[pl.ds(chunk, 512, stride=8), :].reshape(2, 256, 128)
         m[:, chunk // 2, :, pl.ds(chunk % 2 * 128, 128)] = part
     lane = lax.broadcasted_iota(jnp.int32, (8, 128), 1)
-    for half in range(2):
-        for dy, dk in ((0, 0), *COLUMN):
-            place = children.arrive(half, dy, dk)
-            spot = jnp.where(lane == me.r, landed_spots[place], 0)
-            spot = jnp.sum(spot.astype(F32), keepdims=True).astype(jnp.int32)
-
-            def add(slot, carry, place=place, spot=spot):
-                m[slot // 4, slot % 4] += jnp.where(spot == slot, landed[place], 0.0)
+    first_half = children.first_half()
+    for half in (first_half, 1 - first_half):
+        for group in (((0, 0), *COLUMN[:3]), COLUMN[3:]):
+            places = [children.arrive(half, dy, dk) for dy, dk in group]
+            spot = []
+            for place in places:
+                mine = jnp.where(lane == me.r, landed_spots[place], 0)
+                spot.append(jnp.sum(mine.astype(F32), keepdims=True).astype(jnp.int32))
+
+            def add(slot, carry, places=places, spot=spot):
+                parts = [jnp.where(s == slot, landed[p], 0.0) for s, p in zip(spot, places)]
+                m[slot // 4, slot % 4] += (parts[0] + parts[1]) + (parts[2] + parts[3])
                 return carry
 
             lax.fori_loop(0, 8, add, 0)
@@ -582,7 +598,7 @@
             DMA((8,)), [DMA((2,)), DMA((2,))] + [DMA((16,))] * 8,
         ],
         compiler_params=pltpu.CompilerParams(
-            collective_id=0, has_side_effects=True, vmem_limit_bytes=56 * 2**20
+            collective_id=0, has_side_effects=True, vmem_limit_bytes=44 * 2**20
         ),
     )(panel, targets, front, tiles)[0]
 

time: 163 us -> 163 us (level)
  local copies, waits for them, and re-layouts: 0 us -> 4.27 us
  Pallas kernels: 162 us -> 158 us
    pallas_call x1, Pallas kernels: 159 us -> 155 us  [eliminate(): pl.pallas_call(pivot_kernel, name='pivots', out_shape=[jax.ShapeDtypeStru...]
    unnamed x0 -> x8, local copies, waits for them, and re-layouts: none -> 4.27 us
where the time goes in v4:
time: 163 us; the launch traced here: 162 us
  Pallas kernels  158 us (97%)
  local copies, waits for them, and re-layouts  4.27 us (3%)
    pallas_call x1, Pallas kernels, eliminate(): pl.pallas_call(pivot_kernel, name='pivots', out_shape=[jax.ShapeDtypeStru...  155 us
    unnamed x8, local copies, waits for them, and re-layouts  4.27 us

profile of v4, /device:TPU:1, one launch (start us, length us, event | category | flops | bytes accessed | tf_op | source)
XLA Modules:
  0.0 162.0 jit_solution(18170964553069241402)
XLA Ops:
  0.0 0.0 copy-start
  0.0 1.6 copy-done
  1.6 0.0 copy-start.2
  1.6 0.7 copy-done.2
  2.3 0.0 copy-start.3
  2.3 0.7 copy-done.3
  3.0 154.6 %pivots.1 = (f32[4096,128]{1,0:T(8,128)S(1)}, f32[16,256,256]{2,1,0:T(8,128)}, s32[16,8,128]{2,1,0:T(8,128)}) custom-call(s32[2,2]{1,0:T(2,128)S(1)} %copy-done.2, s32[2,16]{1,0:T(2,128)S(1)} %bitcast.7, f32[4096,128]{1,0:T(8,128)S(1)} %bitcast.6, f32[16,256,256]{2,1,0:T(8,128)} %bitcast.8), custom_call_target="tpu_custom_call" | custom-call | tf_op jit(solution)/shard_map/pivots/pallas_call | solution.py:565
  157.5 0.0 copy-start.1
  157.5 1.3 copy-done.1
  158.8 3.0 %hand_over.1 = f32[4096,128]{1,0:T(8,128)} custom-call(f32[4096,128]{1,0:T(8,128)} %copy-done.1), custom_call_target="tpu_custom_call" | custom-call | tf_op jit(solution)/shard_map/hand_over/pallas_call | solution.py:618
Async XLA Ops:
  0.0 1.6 copy-start
  1.6 0.7 copy-start.2
  2.3 0.7 copy-start.3
  157.5 1.3 copy-start.1

commit v5 on v4

--- a/solution.py
+++ b/solution.py
@@ -286,7 +286,7 @@
 
 
 def pivot_kernel(
-    panel, targets, front, tiles, out, mid, mid_spots, spots, landed, landed_spots, m, result, rows, cols, ug, bg, cg, upc, cpc, bsc, bpc,
+    panel, targets, front_in, tiles, out, mid_spots, mid, spots, landed, landed_spots, m, front, result, rows, cols, ug, bg, cg, upc, cpc, bsc, bpc,
     block, block_high, block_low, x1, x2, l1, l2, c2, lt_high, lt_low, own,
     row_s, row_r, col_s, col_r, bs_s, bs_r, bc_s, bc_r, c_s, c_r, cx_s, cx_r, ua, ub, ba, bb, bx_s, bx_r,
     out_sem, child_sems,
@@ -298,7 +298,15 @@
     spots[...] = jnp.zeros_like(spots)
     spots[0:1, 0:16] = targets[0:1, :] // 16 * 4 + targets[1:2, :] // 8
     children = Children(me, tiles, spots, mid, mid_spots, landed, landed_spots, child_sems)
+    brought = [
+        pltpu.make_async_copy(front_in.at[pl.ds(512 * i, 512)], front.at[pl.ds(512 * i, 512)], out_sem.at[i])
+        for i in range(8)
+    ]
     children.send()
+    for copy in brought:
+        copy.start()
+    for copy in brought:
+        copy.wait()
     for chunk in range(8):
         part = front[pl.ds(chunk, 512, stride=8), :].reshape(2, 256, 128)
         m[:, chunk // 2, :, pl.ds(chunk % 2 * 128, 128)] = part
@@ -567,16 +575,17 @@
         name="pivots",
         out_shape=[
             jax.ShapeDtypeStruct((4096, 128), F32),
-            jax.ShapeDtypeStruct((16, 256, 256), F32),
             jax.ShapeDtypeStruct((16, 8, 128), jnp.int32),
         ],
-        in_specs=[SMEM, VMEM, VMEM, ANY],
-        out_specs=[ANY] * 3,
+        in_specs=[SMEM, VMEM, ANY, ANY],
+        out_specs=[ANY] * 2,
         scratch_shapes=[
+            pltpu.VMEM((16, 256, 256), F32),
             pltpu.VMEM((8, 128), jnp.int32),
             pltpu.VMEM((16, 256, 256), F32),
             pltpu.VMEM((16, 8, 128), jnp.int32),
             pltpu.VMEM((2, 4, 256, 256), F32),
+            pltpu.VMEM((4096, 128), F32),
             pltpu.VMEM((4096, 128), F32),
             pltpu.VMEM((16, 2, 4, 16, 256), F32),
             pltpu.VMEM((8, 4, 64, 256), F32),
@@ -598,19 +607,24 @@
             DMA((8,)), [DMA((2,)), DMA((2,))] + [DMA((16,))] * 8,
         ],
         compiler_params=pltpu.CompilerParams(
-            collective_id=0, has_side_effects=True, vmem_limit_bytes=44 * 2**20
+            collective_id=0, has_side_effects=True, vmem_limit_bytes=56 * 2**20
         ),
     )(panel, targets, front, tiles)[0]
 
 
-def hand_over_kernel(source, out, sems):
-    copies = [
-        pltpu.make_async_copy(source.at[pl.ds(512 * i, 512)], out.at[pl.ds(512 * i, 512)], sems.at[i])
-        for i in range(8)
-    ]
-    for copy in copies:
+def hand_over_kernel(source, out, held, sems):
+    def copies(step):
+        refs = ((source, held), (held, out))[step]
+        for i in range(8):
+            part = pl.ds(4096 // 8 * i, 4096 // 8)
+            yield pltpu.make_async_copy(refs[0].at[part], refs[1].at[part], sems.at[step, i])
+
+    for copy in copies(0):
         copy.start()
-    for copy in copies:
+    for brought, written in zip(copies(0), copies(1)):
+        brought.wait()
+        written.start()
+    for copy in copies(1):
         copy.wait()
 
 
@@ -619,9 +633,10 @@
         hand_over_kernel,
         name="hand_over",
         out_shape=jax.ShapeDtypeStruct(result.shape, result.dtype),
-        in_specs=[VMEM],
+        in_specs=[ANY],
         out_specs=ANY,
-        scratch_shapes=[DMA((8,))],
+        scratch_shapes=[pltpu.VMEM(result.shape, result.dtype), DMA((2, 8))],
+        compiler_params=pltpu.CompilerParams(vmem_limit_bytes=60 * 2**20),
     )(result)
 
 

time: 163 us -> 157 us (0.963)
  local copies, waits for them, and re-layouts: 4.27 us -> 0 us
    unnamed x8 -> x0, local copies, waits for them, and re-layouts: 4.27 us -> none
where the time goes in v5:
time: 157 us
  Pallas kernels  157 us (100%)
    pallas_call x1, Pallas kernels, eliminate(): pl.pallas_call(pivot_kernel, name='pivots', out_shape=[jax.ShapeDtypeStru...  154 us

profile of v5, /device:TPU:1, one launch (start us, length us, event | category | flops | bytes accessed | tf_op | source)
XLA Modules:
  0.0 156.8 jit_solution(687949835645426740)
XLA Ops:
  0.0 154.3 %pivots.1 = (f32[4096,128]{1,0:T(8,128)}, s32[16,8,128]{2,1,0:T(8,128)}) custom-call(s32[2,2]{1,0:T(2,128)} %panel.1, s32[2,16]{1,0:T(2,128)} %bitcast.8, f32[4096,128]{1,0:T(8,128)} %bitcast.7, f32[16,256,256]{2,1,0:T(8,128)} %bitcast.6), custom_call_target="tpu_custom_call" | custom-call | tf_op jit(solution)/shard_map/pivots/pallas_call | solution.py:573
  154.3 2.4 %hand_over.1 = f32[4096,128]{1,0:T(8,128)} custom-call(f32[4096,128]{1,0:T(8,128)} %get-tuple-element.6.source), custom_call_target="tpu_custom_call" | custom-call | tf_op jit(solution)/shard_map/hand_over/pallas_call | solution.py:632

commit v6 on v5

--- a/solution.py
+++ b/solution.py
@@ -429,8 +429,8 @@
     def b_at(pivot):
         return lambda source: bg.at[:, pivot, source]
 
-    b1 = PlaneGather(me, b_at(me.k), b_at(me.k)(me.r), True, False, ba)
-    b2 = PlaneGather(me, b_at(2 + me.k), b_at(2 + me.k)(me.r), False, False, bb)
+    b1 = PlaneGather(me, b_at(me.k), b_at(me.k)(me.r), True, True, ba)
+    b2 = PlaneGather(me, b_at(2 + me.k), b_at(2 + me.k)(me.r), False, True, bb)
     b1.start()
     b2.start()
 
@@ -454,18 +454,16 @@
             source = gather.forward(which)
             b_swap(half, which - 1, source, False).start()
     for which in range(4):
-        for gather in (u1, u2):
-            gather.forward(which)
-    for which in range(4):
         for half, gather in enumerate((b1, b2)):
             for index, source in enumerate(gather.relay_second(which)):
                 b_swap(half, 3 + which * 3 + index, source, False).start()
+    for which in range(4):
+        for gather in (u1, u2):
+            gather.forward(which)
     for which in range(1, 4):
         source = me.col(-STEP[which - 1], 0)
         c_out(which - 1)(source).wait_recv()
         c_swap(which)(source).start()
-    for gather in (u1, u2):
-        gather.relay_second(0)
     for half, gather in enumerate((b1, b2)):
         for which in range(4):
             source = gather.finish(which)
@@ -498,15 +496,14 @@
 
     b_arrived(0, b1)
     block[...] = b_part(0, 0)
-    u_relay(1)
     invert(block, block_high, block_low, x1)
+    u_relay(0)
     b_arrived(1, b2)
-    u_relay(2)
     x1_halves = split(x1[...])
     b12 = split(b_part(0, 1))
     t_halves = split(dot3(split(b_part(1, 0)), x1_halves))
     block[...] = b_part(1, 1) - dot3(t_halves, b12)
-    u_relay(3)
+    u_relay(1)
     own_c.wait()
     for which in range(4):
         c_swap(which)(me.col(-STEP[which - 1] if which else 0, 1)).wait_recv()
@@ -514,6 +511,8 @@
     l1[...] = lower
     lower = jnp.where(in1, 0.0, lower)
     c2[...] = c_part(1) - dot3(split(lower), b12)
+    u_relay(2)
+    u_relay(3)
     invert(block, block_high, block_low, x2)
     lower2 = dot3(split(c2[...]), split(x2[...]))
     l2[...] = lower2

time: 157 us -> 151 us (0.962)
  Pallas kernels: 157 us -> 151 us
    pallas_call x1, Pallas kernels: 154 us -> 149 us  [eliminate(): pl.pallas_call(pivot_kernel, name='pivots', out_shape=[jax.ShapeDtypeStru...]
where the time goes in v6:
time: 151 us
  Pallas kernels  151 us (100%)
    pallas_call x1, Pallas kernels, eliminate(): pl.pallas_call(pivot_kernel, name='pivots', out_shape=[jax.ShapeDtypeStru...  149 us

profile of v6, /device:TPU:1, one launch (start us, length us, event | category | flops | bytes accessed | tf_op | source)
XLA Modules:
  0.0 151.2 jit_solution(7492263585672915237)
XLA Ops:
  0.0 148.6 %pivots.1 = (f32[4096,128]{1,0:T(8,128)}, s32[16,8,128]{2,1,0:T(8,128)}) custom-call(s32[2,2]{1,0:T(2,128)} %panel.1, s32[2,16]{1,0:T(2,128)} %bitcast.8, f32[4096,128]{1,0:T(8,128)} %bitcast.7, f32[16,256,256]{2,1,0:T(8,128)} %bitcast.6), custom_call_target="tpu_custom_call" | custom-call | tf_op jit(solution)/shard_map/pivots/pallas_call | solution.py:572
  148.7 2.4 %hand_over.1 = f32[4096,128]{1,0:T(8,128)} custom-call(f32[4096,128]{1,0:T(8,128)} %get-tuple-element.6.source), custom_call_target="tpu_custom_call" | custom-call | tf_op jit(solution)/shard_map/hand_over/pallas_call | solution.py:631

commit v7 on v6

--- a/solution.py
+++ b/solution.py
@@ -447,12 +447,14 @@
     own_c = pltpu.make_async_copy(cpc, cg.at[me.c], own.at[5])
     own_c.start()
 
-    for gather in (u1, u2, b1, b2):
+    for gather in (b1, b2):
         gather.relay()
     for which in range(1, 4):
         for half, gather in enumerate((b1, b2)):
             source = gather.forward(which)
             b_swap(half, which - 1, source, False).start()
+    for gather in (u1, u2):
+        gather.relay()
     for which in range(4):
         for half, gather in enumerate((b1, b2)):
             for index, source in enumerate(gather.relay_second(which)):

time: 151 us -> 151 us (level)
  no operation moved by 1% of the time
where the time goes in v7:
time: 151 us
  Pallas kernels  151 us (100%)
    pallas_call x1, Pallas kernels, eliminate(): pl.pallas_call(pivot_kernel, name='pivots', out_shape=[jax.ShapeDtypeStru...  149 us

profile of v7, /device:TPU:1, one launch (start us, length us, event | category | flops | bytes accessed | tf_op | source)
XLA Modules:
  0.0 151.2 jit_solution(12911869290928373350)
XLA Ops:
  0.0 148.6 %pivots.1 = (f32[4096,128]{1,0:T(8,128)}, s32[16,8,128]{2,1,0:T(8,128)}) custom-call(s32[2,2]{1,0:T(2,128)} %panel.1, s32[2,16]{1,0:T(2,128)} %bitcast.8, f32[4096,128]{1,0:T(8,128)} %bitcast.7, f32[16,256,256]{2,1,0:T(8,128)} %bitcast.6), custom_call_target="tpu_custom_call" | custom-call | tf_op jit(solution)/shard_map/pivots/pallas_call | solution.py:574
  148.7 2.4 %hand_over.1 = f32[4096,128]{1,0:T(8,128)} custom-call(f32[4096,128]{1,0:T(8,128)} %get-tuple-element.6.source), custom_call_target="tpu_custom_call" | custom-call | tf_op jit(solution)/shard_map/hand_over/pallas_call | solution.py:633

commit v8 on v7

--- a/solution.py
+++ b/solution.py
@@ -499,8 +499,8 @@
     b_arrived(0, b1)
     block[...] = b_part(0, 0)
     invert(block, block_high, block_low, x1)
+    b_arrived(1, b2)
     u_relay(0)
-    b_arrived(1, b2)
     x1_halves = split(x1[...])
     b12 = split(b_part(0, 1))
     t_halves = split(dot3(split(b_part(1, 0)), x1_halves))

time: 151 us -> 151 us (level)
  no operation moved by 1% of the time
where the time goes in v8:
time: 151 us
  Pallas kernels  151 us (100%)
    pallas_call x1, Pallas kernels, eliminate(): pl.pallas_call(pivot_kernel, name='pivots', out_shape=[jax.ShapeDtypeStru...  149 us

profile of v8, /device:TPU:1, one launch (start us, length us, event | category | flops | bytes accessed | tf_op | source)
XLA Modules:
  0.0 151.2 jit_solution(7834829360793462002)
XLA Ops:
  0.0 148.6 %pivots.1 = (f32[4096,128]{1,0:T(8,128)}, s32[16,8,128]{2,1,0:T(8,128)}) custom-call(s32[2,2]{1,0:T(2,128)} %panel.1, s32[2,16]{1,0:T(2,128)} %bitcast.8, f32[4096,128]{1,0:T(8,128)} %bitcast.7, f32[16,256,256]{2,1,0:T(8,128)} %bitcast.6), custom_call_target="tpu_custom_call" | custom-call | tf_op jit(solution)/shard_map/pivots/pallas_call | solution.py:574
  148.6 2.4 %hand_over.1 = f32[4096,128]{1,0:T(8,128)} custom-call(f32[4096,128]{1,0:T(8,128)} %get-tuple-element.6.source), custom_call_target="tpu_custom_call" | custom-call | tf_op jit(solution)/shard_map/hand_over/pallas_call | solution.py:633
